TPU v7x, 32 devices: a whole 2x2x4 slice. The times are simulated.
32 devices in a mesh: dp: 16 (over z, y, x), mp: 2 (over core).
Axes of the slice: x: 2, y: 2, z: 4, core: 2. Of those that a mesh axis runs over, the one named last changes fastest.
Arguments:
- tokens: bfloat16 [8192, 768], P('dp'), may hold values from -6 to 6
- out_grad: bfloat16 [8192, 128], P('dp', 'mp'), may hold values from -6 to 6
- doc_lengths: int32 [16], P('dp'), may hold values from 40 to 512, as said below
- owner_list: int32 [96], replicated, may hold values from 0 to 15, as said below
- bucket_table: int32 [1023], replicated, may hold values from 0 to 31
- unit_weight: float32 [208, 128, 768], P('dp', None, 'mp'), as said below
- unit_first: float32 [208, 128, 768], P('dp', None, 'mp'), as said below
- unit_second: float32 [208, 128, 768], P('dp', None, 'mp'), as said below
- gain_weight: float32 [3, 768], replicated, may hold values from 0.5 to 1.5
- gain_first: float32 [3, 768], replicated, may hold values from -192 to 192
- gain_second: float32 [3, 768], replicated, may hold values from 1170 to 4681
- bias_weight: float32 [32, 12], P(None, 'mp'), may hold values from -3 to 3
- bias_first: float32 [32, 12], P(None, 'mp'), may hold values from -192 to 192
- bias_second: float32 [32, 12], P(None, 'mp'), may hold values from 910 to 3640
- proj_weight: float32 [768, 128], P(None, 'mp'), may hold values from -0.21875 to 0.21875
- proj_first: float32 [768, 128], P(None, 'mp'), may hold values from -448 to 448
- proj_second: float32 [768, 128], P(None, 'mp'), may hold values from 5734 to 22937
Outputs:
- encoded: float32 [8192, 128], P('dp', 'mp')
- token_grad: float32 [8192, 768], P('dp')
- unit_weights: float32 [208, 128, 768], P('dp', None, 'mp')
- unit_firsts: float32 [208, 128, 768], P('dp', None, 'mp')
- unit_seconds: float32 [208, 128, 768], P('dp', None, 'mp')
- unit_copies: bfloat16 [208, 128, 768], P('dp', None, 'mp')
- gain_weights: float32 [3, 768], replicated
- gain_firsts: float32 [3, 768], replicated
- gain_seconds: float32 [3, 768], replicated
- bias_weights: float32 [32, 12], P(None, 'mp')
- bias_firsts: float32 [32, 12], P(None, 'mp')
- bias_seconds: float32 [32, 12], P(None, 'mp')
- proj_weights: float32 [768, 128], P(None, 'mp')
- proj_firsts: float32 [768, 128], P(None, 'mp')
- proj_seconds: float32 [768, 128], P(None, 'mp')
Inputs may be any that keep to these rules, and one draw needn't show every extreme that they name: A document's tokens fill the first doc_lengths places of its slot of 512; some document has exactly 512 in every draw. `owner_list`: no dp index owns more than 13 units, and one owns exactly 13 in every draw. `unit_weight`: slot d * 13 + j holds the j-th unit, in unit order, of those that owner_list gives to dp index d; other slots hold values that take part in the update only. `unit_first`: laid out in slots as unit_weight. `unit_second`: laid out in slots as unit_weight; positive.
All inputs are finite; a program needn't handle non-finite values.
Results may differ from a plain program's by a relative error of at most 0.015.
The roundings to bfloat16 on the way count: a program that leaves them out, or rounds other values in their place, can miss the bound.
Values may be sent and summed in bfloat16 or wider, within the bound.
No kernel may reach another device: no remote copies, remote signals or barrier semaphores. Data moves between devices by JAX's collectives and lax.ppermute only.
A program may use at most 448 MiB of HBM per device.

v0:
```python
import jax
import jax.numpy as jnp
from jax import lax
from jax.sharding import PartitionSpec as P

D = 768
HEAD_DIM = 64
FF = 3072
BUCKETS = 32
SLOT = 512
UROWS = 128
STEP = 5


NORM_EPS = 1e-06
ADAM_EPS = 1e-08
BETA_ONE = 0.5
BETA_TWO = 0.5
DECAY = 0.01
RATE_MATRIX = 0.02
RATE_SMALL = 0.1
RATE_GAIN = 0.6
GELU_C = 0.7978845608
GELU_K = 0.044715
MASKED = -1000000000.0


def gelu_tanh(values):
    return 0.5 * values * (1.0 + jnp.tanh(GELU_C * (values + GELU_K * values * values * values)))


def gate_mix(gate_value, upward):
    return gelu_tanh(gate_value) * upward


def inverse_rms(values):
    return lax.rsqrt(jnp.mean(values * values, axis=-1, keepdims=True) + NORM_EPS)


def rms_norm(values, gain_row):
    return values * inverse_rms(values) * gain_row


def norm_back(values, gain_row, grad_in):
    inv_rms = inverse_rms(values)
    weighted = grad_in * gain_row
    gain_grad = jnp.sum(grad_in * values * inv_rms, axis=0)
    values_grad = inv_rms * weighted - values * (inv_rms * inv_rms * inv_rms) * jnp.mean(
        weighted * values, axis=-1, keepdims=True
    )
    return (values_grad, gain_grad)


def plain_dot(left_side, right_side):
    return jnp.dot(left_side, right_side, preferred_element_type=jnp.float32)


def precise_dot(left_side, right_side):
    return jnp.dot(
        left_side, right_side, precision=lax.Precision.HIGHEST, preferred_element_type=jnp.float32
    )


def contract_first(left_side, right_side):
    return lax.dot_general(
        left_side, right_side, (((0,), (0,)), ((), ())), preferred_element_type=jnp.float32
    )


def contract_last(left_side, right_side):
    return lax.dot_general(
        left_side, right_side, (((1,), (1,)), ((), ())), preferred_element_type=jnp.float32
    )


def adamw_step(weight_now, first_now, second_now, grad_in, rate):
    first_new = BETA_ONE * first_now + (1.0 - BETA_ONE) * grad_in
    second_new = BETA_TWO * second_now + (1.0 - BETA_TWO) * grad_in * grad_in
    first_hat = first_new / (1.0 - BETA_ONE**STEP)
    second_hat = second_new / (1.0 - BETA_TWO**STEP)
    weight_new = weight_now - rate * (
        first_hat / (jnp.sqrt(second_hat) + ADAM_EPS) + DECAY * weight_now
    )
    return (weight_new, first_new, second_new)


def shards(
    tokens,
    out_grad,
    doc_lengths,
    owner_list,
    bucket_table,
    unit_weight,
    unit_first,
    unit_second,
    gain_weight,
    gain_first,
    gain_second,
    bias_weight,
    bias_first,
    bias_second,
    proj_weight,
    proj_first,
    proj_second,
):
    own_most = unit_weight.shape[0]
    half_width = unit_weight.shape[2]
    local_heads = bias_weight.shape[1]
    doc_count = doc_lengths.shape[0]
    token_count = tokens.shape[0]
    unit_count = owner_list.shape[0]
    row_count = D // UROWS
    blocks = FF // D
    devices = lax.axis_size("dp")
    indices = jnp.arange(unit_count, dtype=jnp.int32)
    earlier = (owner_list[:, None] == owner_list[None, :]) & (indices[None, :] < indices[:, None])
    unit_rank = jnp.sum(earlier.astype(jnp.int32), axis=1)
    slot_of = owner_list * own_most + unit_rank
    slot_ids = jnp.arange(devices * own_most, dtype=jnp.int32)
    matches = slot_of[None, :] == slot_ids[:, None]
    slot_unit = jnp.sum(jnp.where(matches, indices[None, :], 0), axis=1)
    slot_full = jnp.any(matches, axis=1)
    forward_slots = unit_weight.astype(jnp.bfloat16)
    every_slot = lax.all_gather(forward_slots, "dp", axis=0, tiled=True)
    forward_units = jnp.take(every_slot, slot_of, axis=0)

    def square(first_unit):
        return forward_units[first_unit : first_unit + row_count].reshape(D, half_width)

    def wide_matrix(first_unit):
        pieces = forward_units[first_unit : first_unit + row_count * blocks].reshape(
            row_count, blocks, UROWS, half_width
        )
        return pieces.transpose(0, 2, 1, 3).reshape(D, blocks * half_width)

    offset = 4 * row_count
    stride = row_count * blocks
    query_weight = square(0)
    key_weight = square(row_count)
    value_weight = square(2 * row_count)
    out_weight = square(3 * row_count)
    gate_weight = wide_matrix(offset)
    up_weight = wide_matrix(offset + stride)
    down_weight = wide_matrix(offset + 2 * stride)
    places = jnp.arange(SLOT, dtype=jnp.int32)
    relative = places[None, :] - places[:, None] + SLOT - 1
    bucket_hot = (bucket_table[:, None] == jnp.arange(BUCKETS, dtype=jnp.int32)[None, :]).astype(
        jnp.float32
    )
    by_offset = precise_dot(bucket_hot, bias_weight)
    score_bias = jnp.take(by_offset.T, relative, axis=1)
    valid_keys = places[None, :] < doc_lengths[:, None]

    def split_heads(values):
        return values.reshape(doc_count, SLOT, local_heads, HEAD_DIM)

    def scores_of(query_doc, key_doc, valid_doc):
        scores = (
            jnp.einsum("qhd,khd->hqk", query_doc, key_doc, preferred_element_type=jnp.float32)
            + score_bias
        )
        return jnp.where(valid_doc[None, None, :], scores, MASKED)

    inputs = tokens.astype(jnp.float32)
    first_in = rms_norm(inputs, gain_weight[0]).astype(jnp.bfloat16)
    queries = plain_dot(first_in, query_weight).astype(jnp.bfloat16)
    key_proj = plain_dot(first_in, key_weight).astype(jnp.bfloat16)
    value_proj = plain_dot(first_in, value_weight).astype(jnp.bfloat16)

    def attend(doc_item):
        query_doc, key_doc, value_doc, valid_doc = doc_item
        scores = scores_of(query_doc, key_doc, valid_doc)
        row_max = jnp.max(scores, axis=-1, keepdims=True)
        row_total = jnp.sum(jnp.exp(scores - row_max), axis=-1, keepdims=True)
        log_total = row_max + jnp.log(row_total)
        weights = jnp.exp(scores - log_total).astype(jnp.bfloat16)
        mixed_doc = jnp.einsum(
            "hqk,khd->qhd", weights, value_doc, preferred_element_type=jnp.float32
        )
        return (mixed_doc.astype(jnp.bfloat16), log_total)

    mixed_heads, log_totals = lax.map(
        attend, (split_heads(queries), split_heads(key_proj), split_heads(value_proj), valid_keys)
    )
    mixed_flat = mixed_heads.reshape(token_count, half_width)
    attn_out = lax.psum(contract_last(mixed_flat, out_weight), "mp")
    residual_one = inputs + attn_out
    second_in = rms_norm(residual_one, gain_weight[1]).astype(jnp.bfloat16)
    gate_value = plain_dot(second_in, gate_weight)
    upward = plain_dot(second_in, up_weight)
    hidden = gate_mix(gate_value, upward).astype(jnp.bfloat16)
    feed_out = lax.psum(contract_last(hidden, down_weight), "mp")
    residual_two = residual_one + feed_out
    third_in = rms_norm(residual_two, gain_weight[2]).astype(jnp.bfloat16)
    proj_low = proj_weight.astype(jnp.bfloat16)
    encoded = plain_dot(third_in, proj_low)
    rowmask = valid_keys.reshape(-1)
    out_low = jnp.where(rowmask[:, None], out_grad, jnp.zeros_like(out_grad))
    proj_grad = contract_first(third_in, out_low)
    third_grad = lax.psum(contract_last(out_low, proj_low), "mp")
    grad_two, gain_three = norm_back(residual_two, gain_weight[2], third_grad)
    feed_grad = grad_two.astype(jnp.bfloat16)
    hidden_grad = plain_dot(feed_grad, down_weight)
    down_grad = contract_first(feed_grad, hidden)
    mix_pull = jax.vjp(gate_mix, gate_value, upward)[1]
    gate_grad, up_grad = mix_pull(hidden_grad)
    gate_grad = gate_grad.astype(jnp.bfloat16)
    up_grad = up_grad.astype(jnp.bfloat16)
    second_grad = lax.psum(
        contract_last(gate_grad, gate_weight) + contract_last(up_grad, up_weight), "mp"
    )
    gate_wgrad = contract_first(second_in, gate_grad)
    up_wgrad = contract_first(second_in, up_grad)
    back_two, gain_two = norm_back(residual_one, gain_weight[1], second_grad)
    grad_one = grad_two + back_two
    attn_grad = grad_one.astype(jnp.bfloat16)
    out_wgrad = contract_first(attn_grad, mixed_flat)
    mixed_grad = plain_dot(attn_grad, out_weight).astype(jnp.bfloat16)

    def attend_back(score_total, doc_item):
        query_doc, key_doc, value_doc, valid_doc, log_total, grad_doc = doc_item
        scores = scores_of(query_doc, key_doc, valid_doc)
        probabilities = jnp.exp(scores - log_total)
        weights = probabilities.astype(jnp.bfloat16)
        prob_grad = jnp.einsum(
            "qhd,khd->hqk", grad_doc, value_doc, preferred_element_type=jnp.float32
        )
        score_grad = (
            probabilities * (prob_grad - jnp.sum(probabilities * prob_grad, axis=-1, keepdims=True))
        ).astype(jnp.bfloat16)
        value_grad = jnp.einsum(
            "hqk,qhd->khd", weights, grad_doc, preferred_element_type=jnp.float32
        )
        query_grad = jnp.einsum(
            "hqk,khd->qhd", score_grad, key_doc, preferred_element_type=jnp.float32
        )
        key_grad = jnp.einsum(
            "hqk,qhd->khd", score_grad, query_doc, preferred_element_type=jnp.float32
        )
        grads_out = (
            query_grad.astype(jnp.bfloat16),
            key_grad.astype(jnp.bfloat16),
            value_grad.astype(jnp.bfloat16),
        )
        return (score_total + score_grad.astype(jnp.float32), grads_out)

    score_start = jnp.zeros((local_heads, SLOT, SLOT), jnp.float32)
    score_total, (query_grads, key_grads, value_grads) = lax.scan(
        attend_back,
        score_start,
        (
            split_heads(queries),
            split_heads(key_proj),
            split_heads(value_proj),
            valid_keys,
            log_totals,
            split_heads(mixed_grad),
        ),
    )
    query_grads = query_grads.reshape(token_count, half_width)
    key_grads = key_grads.reshape(token_count, half_width)
    value_grads = value_grads.reshape(token_count, half_width)
    offset_grad = jax.ops.segment_sum(
        score_total.reshape(local_heads, SLOT * SLOT).T,
        relative.reshape(-1),
        num_segments=2 * SLOT - 1,
    )
    bias_grad = precise_dot(bucket_hot.T, offset_grad)
    first_grad = lax.psum(
        (
            contract_last(query_grads, query_weight)
            + contract_last(key_grads, key_weight)
            + contract_last(value_grads, value_weight)
        ).astype(jnp.bfloat16),
        "mp",
    ).astype(jnp.float32)
    query_wgrad = contract_first(first_in, query_grads)
    key_wgrad = contract_first(first_in, key_grads)
    value_wgrad = contract_first(first_in, value_grads)
    back_one, gain_one = norm_back(inputs, gain_weight[0], first_grad)
    token_grad = grad_one + back_one

    def square_back(grad_in):
        return grad_in.reshape(row_count, UROWS, half_width)

    def wide_back(grad_in):
        return (
            grad_in.reshape(row_count, UROWS, blocks, half_width)
            .transpose(0, 2, 1, 3)
            .reshape(row_count * blocks, UROWS, half_width)
        )

    unit_grad = jnp.concatenate(
        [
            square_back(query_wgrad),
            square_back(key_wgrad),
            square_back(value_wgrad),
            square_back(out_wgrad),
            wide_back(gate_wgrad),
            wide_back(up_wgrad),
            wide_back(down_grad),
        ],
        axis=0,
    )
    gain_total, bias_total, proj_total = lax.psum(
        (jnp.stack([gain_one, gain_two, gain_three]), bias_grad, proj_grad), "dp"
    )
    picked = jnp.take(unit_grad, slot_unit, axis=0)
    owned_grad = lax.psum_scatter(
        jnp.where(slot_full[:, None, None], picked, 0.0), "dp", scatter_dimension=0, tiled=True
    )
    unit_weights, unit_firsts, unit_seconds = adamw_step(
        unit_weight, unit_first, unit_second, owned_grad, RATE_MATRIX
    )
    gain_weights, gain_firsts, gain_seconds = adamw_step(
        gain_weight, gain_first, gain_second, gain_total, RATE_GAIN
    )
    bias_weights, bias_firsts, bias_seconds = adamw_step(
        bias_weight, bias_first, bias_second, bias_total, RATE_SMALL
    )
    proj_weights, proj_firsts, proj_seconds = adamw_step(
        proj_weight, proj_first, proj_second, proj_total, RATE_MATRIX
    )
    return (
        encoded,
        token_grad,
        unit_weights,
        unit_firsts,
        unit_seconds,
        unit_weights.astype(jnp.bfloat16),
        gain_weights,
        gain_firsts,
        gain_seconds,
        bias_weights,
        bias_firsts,
        bias_seconds,
        proj_weights,
        proj_firsts,
        proj_seconds,
    )


def solution(mesh):
    in_specs = (
        P("dp", None),
        P("dp", "mp"),
        P("dp"),
        P(),
        P(),
        P("dp", None, "mp"),
        P("dp", None, "mp"),
        P("dp", None, "mp"),
        P(),
        P(),
        P(),
        P(None, "mp"),
        P(None, "mp"),
        P(None, "mp"),
        P(None, "mp"),
        P(None, "mp"),
        P(None, "mp"),
    )
    out_specs = (
        P("dp", "mp"),
        P("dp", None),
        P("dp", None, "mp"),
        P("dp", None, "mp"),
        P("dp", None, "mp"),
        P("dp", None, "mp"),
        P(),
        P(),
        P(),
        P(None, "mp"),
        P(None, "mp"),
        P(None, "mp"),
        P(None, "mp"),
        P(None, "mp"),
        P(None, "mp"),
    )
    return jax.shard_map(shards, mesh=mesh, in_specs=in_specs, out_specs=out_specs, check_vma=False)
```

profile of v0, /device:TPU:0, one launch (start us, length us, event | category | flops | bytes accessed | tf_op | source)
XLA Modules:
  0.0 2803.4 jit_solution(385449341664079074)
XLA Ops:
  7.2 2.9 convert_element_type.101
  12.7 861.6 %gather_fusion.1 = f32[262144,6]{1,0:T(8,128)} fusion(f32[6,1023]{0,1:T(8,128)S(1)} %copy.90, s32[262144]{0:T(1024)S(1)} %broadcast_clamp_fusion), kind=kCustom, calls=%fused_computation.1 | custom fusion | bytes 13631488 | tf_op jit(solution)/shard_map/jit(_take)/gather | solution.py:151
  874.3 72.1 %copy.92 = f32[512,512,6]{0,1,2:T(8,128)} copy(f32[512,512,6]{2,1,0:T(8,128)} %bitcast.8) | data formatting | bytes 12582912 | tf_op jit(solution)/shard_map/jit(_take)/gather | solution.py:151
  948.6 14.7 gather_fusion
  963.3 8.5 broadcast_select_fusion
  971.8 1.9 fusion.61
  975.7 4.9 fusion.62
  988.3 4.0 fusion.60
  992.4 1.8 copy.96
  996.0 1.8 copy.95
  1003.2 6.2 all-reduce.8.cloned.1.call-done
  1009.5 1.8 multiply_reduce_fusion.6
  1014.1 3.4 multiply_convert_fusion.2
  1017.5 2.6 fusion.65
  1020.3 24.3 all-reduce.16.cloned.1.call-done
  1050.6 4.2 multiply_convert_fusion.1
  1057.6 2.6 convolution_add_fusion
  1063.4 5.0 fusion.29
  1068.5 13.5 all-reduce.10.cloned.1.call-done
  1082.0 2.6 multiply_reduce_fusion.2
  1084.6 2.9 convert_bitcast_fusion
  1091.1 1.9 multiply_convert_fusion
  1098.4 5.2 fusion.70
  1103.6 6.2 reshape.312
  1109.8 5.1 copy.108
  1114.9 6.2 reshape.310
  1121.1 5.3 copy.107
  1126.4 3.6 fusion.69
  1130.0 6.2 reshape.308
  1136.2 5.2 copy.106
  1142.4 2.3 copy.104
  1144.7 2.2 fusion.18
  1147.0 3.4 fusion.51
  1150.4 2.3 copy.100
  1152.7 3.0 convolution_dynamic-update-slice_fusion.3
  1160.6 5.1 constant_dynamic-update-slice_fusion.2
  1165.8 2.9 constant_dynamic-update-slice_fusion.1
  1169.8 2.6 constant_dynamic-update-slice_fusion
  1172.4 32.9 %gather_fusion.2 = f32[208,128,384]{2,1,0:T(8,128)} fusion(f32[96,128,384]{2,1,0:T(8,128)} %constant_dynamic-update-slice_fusion, s32[1024]{0:T(1024)} %pad_clamp_fusion), kind=kCustom, calls=%fused_computation.2 | custom fusion | bytes 81789760 | tf_op jit(solution)/shard_map/jit(_take)/gather | solution.py:308
  1205.2 29.8 %select_select_fusion = f32[208,128,384]{2,1,0:T(8,128)} fusion(f32[208,128,384]{2,1,0:T(8,128)} %gather_fusion.2, pred[208]{0:T(512)(128)(4,1)S(1)} %copy-done.72, pred[208]{0:T(512)(128)(4,1)S(1)} %copy-done.71), kind=kLoop, calls=%fused_computation.4 | loop fusion | flops 20447232 | bytes 81789344 | tf_op jit(solution)/shard_map/jit(_where)/select_n | solution.py:310
  1237.5 13.0 all-reduce.14.cloned.1.call-done
  1250.5 1.9 multiply_subtract_fusion.2
  1252.4 3.5 copy.109
  1255.9 10.2 copy.130
  1266.2 58.6 %copy.110 = f32[262144,6]{1,0:T(8,128)} copy(f32[262144,6]{0,1:T(8,128)} %bitcast.132) | data formatting | bytes 12582912 | tf_op jit(solution)/shard_map/transpose | solution.py:264
  1324.8 1386.5 %scatter_custom_fusion = f32[1023,6]{1,0:T(8,128)S(1)} fusion(s32[262144]{0:T(1024)} %bitcast.182, f32[262144,6]{1,0:T(8,128)} %copy.110, f32[]{:T(128)} %constant.87.clone.1), kind=kCustom, calls=%fused_computation.92 | custom fusion | flops 1572864 | bytes 25064 | tf_op jit(solution)/shard_map/scatter-add | solution.py:263
  2712.1 74.7 %all-reduce = (f32[3,768]{1,0:T(4,128)S(1)}, f32[32,6]{0,1:T(8,128)S(1)}) all-reduce(f32[3,768]{1,0:T(4,128)S(1)} %pad_maximum_fusion, f32[32,6]{0,1:T(8,128)S(1)} %fusion.27), channel_id=1, replica_groups=mesh['dp'=16,'mp'=2] {'dp'}, use_global_device_ids=true, to_apply=%region_21.22 | all-reduce | flops 2496 | bytes 19968 | tf_op jit(solution)/shard_map/psum | solution.py:305
  2788.1 8.3 fusion.58
  (249 shorter events, 56.0 us)
Async XLA Ops:
  7.2 4.2 copy-start.65
  7.2 4.2 copy-start.63
  7.2 941.4 %all-gather.2.cloned.1.call-start = ((), (), s32[]{:S(2)}) async-start(), calls=%async_computation.1 | async-start | bytes 21725184 | tf_op jit(solution)/shard_map/all_gather | solution.py:124
  10.2 999.2 %all-reduce.8.cloned.1.call-start = ((), (), s32[]{:S(2)}) async-start(), calls=%async_computation.2 | async-start | bytes 3145728 | tf_op jit(solution)/shard_map/psum | solution.py:186
  874.3 72.1 %copy-start.69 = (s32[96]{0:T(128)S(1)}, s32[96]{0:T(128)}, u32[]{:S(2)}) copy-start(s32[96]{0:T(128)} %param.20) | copy-start | bytes 1156
  874.3 72.9 %copy-start.47 = (f32[3,768]{1,0:T(4,128)S(1)}, f32[3,768]{1,0:T(4,128)}, u32[]{:S(2)}) copy-start(f32[3,768]{1,0:T(4,128)} %param.25) | copy-start | bytes 27652
  874.3 73.5 %copy-start.3 = (bf16[512,768]{1,0:T(8,128)(2,1)S(1)}, bf16[512,768]{1,0:T(8,128)(2,1)}, u32[]{:S(2)}) copy-start(bf16[512,768]{1,0:T(8,128)(2,1)} %param.17) | copy-start | bytes 2359300
  946.4 40.3 %copy-start.61 = (pred[512]{0:T(512)(128)(4,1)}, pred[512]{0:T(512)(128)(4,1)S(1)}, u32[]{:S(2)}) copy-start(pred[512]{0:T(512)(128)(4,1)S(1)} %iota_compare_fusion.5) | copy-start | bytes 1540
  947.8 27.3 copy-start.49
  947.8 64.1 %copy-start.46 = (f32[768]{0:T(1024)}, f32[768]{0:T(1024)S(1)}, u32[]{:S(2)}) copy-start(f32[768]{0:T(1024)S(1)} %get-tuple-element.82) | copy-start | bytes 9220
  948.6 26.4 copy-start.54
  973.7 10.7 copy-start.11
  974.4 6.3 copy-start.39
  975.0 5.7 copy-start.41
  975.7 5.9 copy-start.33
  986.2 58.4 %all-reduce.16.cloned.1.call-start = ((), (), s32[]{:S(2)}) async-start(), calls=%async_computation.7 | async-start | bytes 6291456 | tf_op jit(solution)/shard_map/psum | solution.py:192
  1013.5 3.9 copy-start.73
  1020.0 26.4 copy-start.51
  1020.1 61.9 %all-reduce.10.cloned.1.call-start = ((), (), s32[]{:S(2)}) async-start(), calls=%async_computation.3 | async-start | bytes 3145728 | tf_op jit(solution)/shard_map/psum | solution.py:209
  1050.6 4.2 copy-start.30
  1060.2 84.5 %all-reduce.12.cloned.1.call-start = ((), (), s32[]{:S(2)}) async-start(), calls=%async_computation.4 | async-start | bytes 1572864 | tf_op jit(solution)/shard_map/psum | solution.py:269
  1082.0 6.6 slice-start
  1084.6 4.0 slice-start.1
  1089.7 6.8 copy-start.13
  1098.1 152.4 %all-reduce.14.cloned.1.call-start = ((), (), s32[]{:S(2)}) async-start(), calls=%async_computation.6 | async-start | bytes 393216 | tf_op jit(solution)/shard_map/psum | solution.py:305
  1121.1 5.3 copy-start.7
  1121.1 5.3 copy-start.36
  1136.2 5.2 copy-start.8
  1136.2 5.2 copy-start.44
  1136.2 5.2 copy-start.62
  1141.4 5.6 copy-start.60
  1142.4 1645.7 %reduce-scatter.2.cloned.1.call-start = ((), (), s32[]{:S(2)}) async-start(), calls=%async_computation.5 | async-start | bytes 43450368 | tf_op jit(solution)/shard_map/reduce_scatter | solution.py:309
  1152.7 4.6 copy-start.14
  1160.6 5.1 slice-start.4
  1160.6 5.1 slice-start.5
  1165.8 3.9 slice-start.2
  1165.8 4.0 slice-start.3
  1172.4 32.9 %copy-start.71 = (pred[208]{0:T(512)(128)(4,1)S(1)}, pred[208]{0:T(512)(128)(4,1)}, u32[]{:S(2)}) copy-start(pred[208]{0:T(512)(128)(4,1)} %fusion.38) | copy-start | bytes 628
  1172.4 32.9 %copy-start.72 = (pred[208]{0:T(512)(128)(4,1)S(1)}, pred[208]{0:T(512)(128)(4,1)}, u32[]{:S(2)}) copy-start(pred[208]{0:T(512)(128)(4,1)} %compare_and_fusion) | copy-start | bytes 628
  1235.1 15.4 copy-start.45
  1266.1 1445.2 %copy-start.64 = (s32[1023]{0:T(1024)S(1)}, s32[1023]{0:T(1024)}, u32[]{:S(2)}) copy-start(s32[1023]{0:T(1024)} %param.21) | copy-start | bytes 12280
  1266.1 1520.7 %copy-start.66 = (f32[32,6]{0,1:T(8,128)S(1)}, f32[32,6]{0,1:T(8,128)}, u32[]{:S(2)}) copy-start(f32[32,6]{0,1:T(8,128)} %param.28) | copy-start | bytes 2308
  1266.1 1520.7 %copy-start.67 = (f32[32,6]{0,1:T(8,128)S(1)}, f32[32,6]{0,1:T(8,128)}, u32[]{:S(2)}) copy-start(f32[32,6]{0,1:T(8,128)} %param.29) | copy-start | bytes 2308
  1266.1 1520.7 %copy-start.68 = (f32[32,6]{0,1:T(8,128)S(1)}, f32[32,6]{0,1:T(8,128)}, u32[]{:S(2)}) copy-start(f32[32,6]{0,1:T(8,128)} %param.30) | copy-start | bytes 2308
  1266.2 1521.3 %copy-start.48 = (f32[3,768]{1,0:T(4,128)S(1)}, f32[3,768]{1,0:T(4,128)}, u32[]{:S(2)}) copy-start(f32[3,768]{1,0:T(4,128)} %param.25) | copy-start | bytes 27652
  1266.2 1521.3 %copy-start.58 = (f32[3,768]{1,0:T(4,128)S(1)}, f32[3,768]{1,0:T(4,128)}, u32[]{:S(2)}) copy-start(f32[3,768]{1,0:T(4,128)} %param.26) | copy-start | bytes 27652
  1266.2 1521.3 %copy-start.59 = (f32[3,768]{1,0:T(4,128)S(1)}, f32[3,768]{1,0:T(4,128)}, u32[]{:S(2)}) copy-start(f32[3,768]{1,0:T(4,128)} %param.27) | copy-start | bytes 27652
  1266.2 1521.9 %copy-start.5 = (f32[13,128,384]{2,1,0:T(8,128)S(1)}, f32[13,128,384]{2,1,0:T(8,128)}, u32[]{:S(2)}) copy-start(f32[13,128,384]{2,1,0:T(8,128)} %param.22) | copy-start | bytes 7667716
  (41 other events, 86.0 us)
Sparse Core Ops, SparseCore 0:
  11.4 229.1 all-gather.1
  986.3 23.0 all-reduce.7
  1020.2 24.4 all-reduce.15
  1060.3 21.5 all-reduce.9
  1098.2 20.3 all-reduce.11
  1142.5 107.9 all-reduce.13
  1257.7 584.3 reduce-scatter.1
where the time goes:
time: 2820 us; the launch traced here: 2800 us
  other arithmetic  1460 us (52%)
  local copies, waits for them, and re-layouts  1130 us (40%)
  blocking collectives  74.7 us (3%)
  matrix products  59 us (2%)
  waiting for transfers between devices  57.2 us (2%)
    scatter-add x1, other arithmetic, shards(): jax.ops.segment_sum(score_total.reshape(local_heads, SLOT * SLOT).T, rela...  1390 us
    gather x2, local copies, waits for them, and re-layouts, shards(): score_bias = jnp.take(by_offset.T, relative, axis=1)  934 us
    psum x1, blocking collectives, shards(): lax.psum((jnp.stack([gain_one, gain_two, gain_three]), bias_grad, proj_gr...  74.7 us
    transpose x2, local copies, waits for them, and re-layouts, shards(): score_total.reshape(local_heads, SLOT * SLOT)  62.1 us
  transfers between devices with their start and end apart: 7, of which 4 were waited for; matrix products, arithmetic and copies ran while one was open for 91% of the time, Pallas kernels for 0%

commit v1 on v0

v1 whole, which is shorter than its diff:
```python
import functools

import jax
import jax.numpy as jnp
from jax import lax
from jax.experimental import pallas as pl
from jax.experimental.pallas import tpu as pltpu
from jax.sharding import PartitionSpec as P

D = 768
HEAD_DIM = 64
FF = 3072
BUCKETS = 32
SLOT = 512
UROWS = 128
STEP = 5
HALF = UROWS // 2

NORM_EPS = 1e-06
ADAM_EPS = 1e-08
BETA_ONE = 0.5
BETA_TWO = 0.5
DECAY = 0.01
RATE_MATRIX = 0.02
RATE_SMALL = 0.1
RATE_GAIN = 0.6
GELU_C = 0.7978845608
GELU_K = 0.044715
MASKED = -1000000000.0

ROWS = D // UROWS
BLOCKS = FF // D
SQUARES = 4 * ROWS
SPREAD = 2 * SLOT
SMALL_TILE = 16
F32 = jnp.float32
BF16 = jnp.bfloat16
ANY = pl.BlockSpec(memory_space=pl.ANY)
SMEM = pl.BlockSpec(memory_space=pltpu.SMEM)
VMEM = pl.BlockSpec(memory_space=pltpu.VMEM)
PAIR = 2 * HEAD_DIM


def dot(left, right):
    return jnp.dot(left, right, preferred_element_type=F32)


def dot_nt(left, right):
    return lax.dot_general(left, right, (((1,), (1,)), ((), ())), preferred_element_type=F32)


def dot_tn(left, right):
    return lax.dot_general(left, right, (((0,), (0,)), ((), ())), preferred_element_type=F32)


def precise_dot(left, right):
    return jnp.dot(left, right, precision=lax.Precision.HIGHEST, preferred_element_type=F32)


def inverse_rms(values):
    return lax.rsqrt(jnp.mean(values * values, axis=-1, keepdims=True) + NORM_EPS)


def norm_back(values, inv_rms, gain_row, grad_in):
    weighted = grad_in * gain_row
    gain_grad = jnp.sum(grad_in * values * inv_rms, axis=0, keepdims=True)
    slope = jnp.mean(weighted * values, axis=-1, keepdims=True)
    values_grad = inv_rms * weighted - values * (inv_rms * inv_rms * inv_rms) * slope
    return values_grad, gain_grad


def adamw_step(weight_now, first_now, second_now, grad_in, rate):
    first_new = BETA_ONE * first_now + (1.0 - BETA_ONE) * grad_in
    second_new = BETA_TWO * second_now + (1.0 - BETA_TWO) * grad_in * grad_in
    first_hat = first_new / (1.0 - BETA_ONE**STEP)
    second_hat = second_new / (1.0 - BETA_TWO**STEP)
    weight_new = weight_now - rate * (
        first_hat / (jnp.sqrt(second_hat) + ADAM_EPS) + DECAY * weight_now
    )
    return weight_new, first_new, second_new


def params(limit_mib):
    return pltpu.CompilerParams(vmem_limit_bytes=limit_mib * 1024 * 1024)


def cost(flops, moved, exps=0):
    return pl.CostEstimate(flops=int(flops), bytes_accessed=int(moved), transcendentals=int(exps))


def ring_order(line):
    return list(range(0, line, 2)) + list(range(line - 1 - line % 2, 0, -2))


def ring_place(z, line):
    return jnp.where(z % 2 == 0, z // 2, line - (z + 1) // 2)


def ring_device(place, line):
    return jnp.where(2 * place < line, 2 * place, 2 * (line - place) - 1)


def hops(devices):
    line = devices // 4
    order = ring_order(line)
    after = {order[i]: order[(i + 1) % line] for i in range(line)}
    along_x = [(i, i ^ 1) for i in range(devices)]
    along_y = [(i, i ^ 2) for i in range(devices)]
    along_z = [(i, after[i // 4] * 4 + i % 4) for i in range(devices)]
    return along_x, along_y, along_z


def send(values, pairs):
    return lax.ppermute(values, "dp", pairs)


def swap(values):
    return lax.ppermute(values, "mp", [(0, 1), (1, 0)])


def unit_place(unit):
    inner = unit - SQUARES
    matrix = inner // (ROWS * BLOCKS)
    rest = inner % (ROWS * BLOCKS)
    wide = SQUARES + matrix * ROWS * BLOCKS + (rest % BLOCKS) * ROWS + rest // BLOCKS
    return jnp.where(unit < SQUARES, unit, wide)


def strays_kernel(own, most, devices, where_ref, weight_ref, keep_a, send_a, keep_b, send_b, stage, sem):
    line = devices // 4
    load = pltpu.make_async_copy(weight_ref.at[own:most], stage, sem)
    load.start()
    for out in (keep_a, send_a, keep_b, send_b):
        out[...] = jnp.zeros_like(out)
    load.wait()
    me = where_ref[0]
    first = where_ref[1]
    count = where_ref[2]
    for j in range(most - own):
        home = first + j

        @pl.when(jnp.logical_and(j < count, home < devices))
        def _():
            rel = jnp.bitwise_xor(home, me)
            rx = jnp.bitwise_and(rel, 1)
            ry = jnp.bitwise_and(rel // 2, 1)
            rz = (ring_place(home // 4, line) - ring_place(me // 4, line) + line) % line
            unit = stage[j].astype(BF16)
            for bit, (here, there) in enumerate(((keep_a, keep_b), (send_a, send_b))):

                @pl.when(rx == bit)
                def _():
                    here[ry, rz] = unit[:HALF]

                @pl.when(ry == bit)
                def _():
                    there[rx, rz] = unit[HALF:]


def assemble_kernel(own, devices, units, extra_count, where_ref, table_ref, *refs):
    line = devices // 4
    *pieces, out_ref, sem, extra_sem = refs
    strays, extra = pieces[8 * line], pieces[8 * line + 1]
    me = where_ref[0]
    slots = own + 1

    def unit_of(rx, ry, rz, slot):
        z = ring_device((ring_place(me // 4, line) - rz + line) % line, line)
        other = z * 4 + jnp.bitwise_xor(me % 4, 2 * ry + rx)
        return table_ref[other * slots + slot]

    for rz in range(line):
        for ry in range(2):
            for rx in range(2):
                block = 8 * rz + 4 * ry + 2 * rx
                for slot in range(own):
                    place = unit_of(rx, ry, rz, slot)
                    for half in range(2):
                        pltpu.make_async_copy(
                            pieces[block + half].at[slot],
                            out_ref.at[place, half * HALF : (half + 1) * HALF],
                            sem,
                        ).start()
                place = unit_of(rx, ry, rz, own)
                pltpu.make_async_copy(
                    strays.at[rz, 2 * ry + rx], out_ref.at[place], sem
                ).start()
    total = devices * slots
    done = 0
    while done < total:
        step = min(units, total - done)
        pltpu.make_async_copy(out_ref.at[0:step], out_ref.at[0:step], sem).wait()
        done += step
    if extra_count:

        @pl.loop(0, where_ref[3])
        def _(i):
            move = pltpu.make_async_copy(
                extra.at[i], out_ref.at[table_ref[devices * slots + i]], extra_sem
            )
            move.start()
            move.wait()


def spread_kernel(own, devices, units, where_ref, table_ref, squares_ref, wides_ref, small_ref, *refs):
    line = devices // 4
    *outs, sem, small_sem = refs
    me = where_ref[0]
    slots = own + 1
    stray_outs = outs[4 * line :]

    def ahead(rx, ry, rz):
        z = ring_device((ring_place(me // 4, line) + rz) % line, line)
        return z * 4 + jnp.bitwise_xor(me % 4, 2 * ry + rx)

    def fetch(place, rows, target):
        bounded = jnp.minimum(place, units - 1)

        @pl.when(bounded < SQUARES)
        def _():
            pltpu.make_async_copy(squares_ref.at[bounded, rows], target, sem).start()

        @pl.when(bounded >= SQUARES)
        def _():
            pltpu.make_async_copy(wides_ref.at[bounded - SQUARES, rows], target, sem).start()

    low, high = pl.ds(0, HALF), pl.ds(HALF, HALF)
    for rz in range(line - 1, -1, -1):
        for ry in range(2):
            for rx in range(2):
                other = ahead(rx, ry, rz)
                for slot in range(own):
                    place = table_ref[other * slots + slot]
                    fetch(place, low, outs[4 * rz + rx].at[ry, slot])
                    fetch(place, high, outs[4 * rz + 2 + ry].at[rx, slot])
                place = table_ref[other * slots + own]
                fetch(place, low, stray_outs[rx].at[ry, rz])
                fetch(place, high, stray_outs[2 + ry].at[rx, rz, low])
                pltpu.make_async_copy(
                    small_ref.at[other],
                    stray_outs[2 + ry].at[rx, rz, pl.ds(HALF, SMALL_TILE)],
                    small_sem,
                ).start()
    total = devices * slots
    done = 0
    while done < total:
        step = min(wides_ref.shape[0], total - done)
        pltpu.make_async_copy(wides_ref.at[0:step], wides_ref.at[0:step], sem).wait()
        done += step
    pltpu.make_async_copy(small_ref, small_ref, small_sem).wait()


def toeplitz(row):
    width = SPREAD
    tile = jnp.broadcast_to(pltpu.roll(row, width - (SLOT - 1), 1), (8, width))
    places = lax.broadcasted_iota(jnp.int32, (8, width), 0)
    for bit in (1, 2, 4):
        tile = jnp.where(jnp.bitwise_and(places, bit) != 0, pltpu.roll(tile, bit, 1), tile)
    reach = 8
    while reach < SLOT // 2:
        tile = jnp.concatenate([tile, pltpu.roll(tile, reach, 1)], axis=0)
        reach *= 2
    lower = jnp.concatenate([tile[:, width - reach :], tile[:, : SLOT - reach]], axis=1)
    return jnp.concatenate([tile[:, :SLOT], lower], axis=0)


def diagonals(tile):
    rows = SLOT
    while rows > 128:
        rows //= 2
        blank = jnp.zeros((rows, rows), F32)
        tile = jnp.concatenate([tile[rows:], blank], axis=1) + jnp.concatenate(
            [blank, tile[:rows]], axis=1
        )
    tile = jnp.concatenate([tile, jnp.zeros((rows, SPREAD - tile.shape[1]), F32)], axis=1)
    while rows > 8:
        rows //= 2
        tile = tile[rows:] + pltpu.roll(tile[:rows], rows, 1)
    places = lax.broadcasted_iota(jnp.int32, tile.shape, 0)
    for bit in (4, 2, 1):
        tile = jnp.where(jnp.bitwise_and(places, bit) == 0, pltpu.roll(tile, bit, 1), tile)
    return jnp.sum(tile, axis=0, keepdims=True)


def matrix(ref, first):
    return ref[first : first + ROWS].reshape(D, ref.shape[2])


def pair_columns(ref, step):
    return ref[:, pl.ds(pl.multiple_of(step * PAIR, PAIR), PAIR)]


def attend_kernel(
    lengths_ref, tokens_ref, gain_ref, weight_ref, bias_ref,
    norm_ref, query_ref, key_ref, value_ref, prob_ref, mixed_ref, part_ref,
):
    step = pl.program_id(0)

    @pl.when(step == 0)
    def _():
        inputs = tokens_ref[...].astype(F32)
        normed = (inputs * inverse_rms(inputs) * gain_ref[0:1, :]).astype(BF16)
        norm_ref[...] = normed
        query_ref[...] = dot(normed, matrix(weight_ref, 0)).astype(BF16)
        key_ref[...] = dot(normed, matrix(weight_ref, ROWS)).astype(BF16)
        value_ref[...] = dot(normed, matrix(weight_ref, 2 * ROWS)).astype(BF16)

    queries = pair_columns(query_ref, step)
    keys = pair_columns(key_ref, step)
    values = pair_columns(value_ref, step)
    lanes = lax.broadcasted_iota(jnp.int32, (SLOT, PAIR), 1) // HEAD_DIM
    seen = lax.broadcasted_iota(jnp.int32, (1, SLOT), 1) < lengths_ref[0]
    mixes = []
    for which in range(2):
        scores = dot_nt(jnp.where(lanes == which, queries, jnp.zeros_like(queries)), keys)
        scores = scores + toeplitz(bias_ref[pl.ds(2 * step + which, 1), :])
        scores = jnp.where(seen, scores, MASKED)
        powers = jnp.exp(scores - jnp.max(scores, axis=-1, keepdims=True))
        probabilities = powers * (1.0 / jnp.sum(powers, axis=-1, keepdims=True))
        prob_ref[which] = probabilities
        mixes.append(dot(probabilities.astype(BF16), values))
    mixed = jnp.where(lanes == 0, mixes[0], mixes[1]).astype(BF16)
    mixed_ref[:, pl.ds(pl.multiple_of(step * PAIR, PAIR), PAIR)] = mixed

    @pl.when(step == pl.num_programs(0) - 1)
    def _():
        part_ref[...] = dot_nt(mixed_ref[...], matrix(weight_ref, 3 * ROWS))


def gelu_tanh(values):
    return jnp.tanh(GELU_C * (values + GELU_K * values * values * values))


def feed_kernel(
    tokens_ref, mine_ref, other_ref, gain_ref, gate_w, up_w, down_w,
    residual_ref, norm_ref, gate_ref, up_ref, hidden_ref, part_ref,
):
    step = pl.program_id(0)

    @pl.when(step == 0)
    def _():
        residual = tokens_ref[...].astype(F32) + (mine_ref[...] + other_ref[...])
        residual_ref[...] = residual
        norm_ref[...] = (residual * inverse_rms(residual) * gain_ref[1:2, :]).astype(BF16)
        part_ref[...] = jnp.zeros_like(part_ref)

    normed = norm_ref[...]
    gate = dot(normed, matrix(gate_w, 0))
    up = dot(normed, matrix(up_w, 0))
    gate_ref[...] = gate
    up_ref[...] = up
    hidden = (0.5 * gate * (1.0 + gelu_tanh(gate)) * up).astype(BF16)
    hidden_ref[...] = hidden
    part_ref[...] += dot_nt(hidden, matrix(down_w, 0))


def turn_kernel(
    lengths_ref, residual_ref, mine_ref, other_ref, gain_ref, proj_ref, proj_other, cot_ref, cot_other,
    gate_ref, up_ref, gate_w, up_w, down_w,
    encoded_ref, proj_grad, gain_grad, grad_ref, feed_ref, dgate_ref, dup_ref, part_ref,
):
    step = pl.program_id(0)

    @pl.when(step == 0)
    def _():
        residual = residual_ref[...] + (mine_ref[...] + other_ref[...])
        inv_rms = inverse_rms(residual)
        normed = (residual * inv_rms * gain_ref[2:3, :]).astype(BF16)
        encoded_ref[...] = dot(normed, proj_ref[...])
        rows = lax.broadcasted_iota(jnp.int32, (SLOT, 1), 0) < lengths_ref[0]
        mine = jnp.where(rows, cot_ref[...], jnp.zeros_like(cot_ref))
        other = jnp.where(rows, cot_other[...], jnp.zeros_like(cot_other))
        backward = dot_tn(mine, normed)
        proj_grad[0] = backward[:, : D // 2]
        proj_grad[1] = backward[:, D // 2 :]
        third = dot_nt(mine, proj_ref[...]) + dot_nt(other, proj_other[...])
        grad, gain = norm_back(residual, inv_rms, gain_ref[2:3, :], third)
        gain_grad[...] = gain
        grad_ref[...] = grad
        feed_ref[...] = grad.astype(BF16)
        part_ref[...] = jnp.zeros_like(part_ref)

    dhidden = dot(feed_ref[...], matrix(down_w, 0))
    gate = gate_ref[...]
    bend = gelu_tanh(gate)
    slope = 0.5 * (1.0 + bend) + 0.5 * gate * (1.0 - bend * bend) * (
        GELU_C * (1.0 + 3.0 * GELU_K * gate * gate)
    )
    dgate = (dhidden * up_ref[...] * slope).astype(BF16)
    dup = (dhidden * (0.5 * gate * (1.0 + bend))).astype(BF16)
    dgate_ref[...] = dgate
    dup_ref[...] = dup
    part_ref[...] += dot_nt(dgate, matrix(gate_w, 0)) + dot_nt(dup, matrix(up_w, 0))


def wide_grads_kernel(norm_ref, feed_ref, hidden_ref, dgate_ref, dup_ref, out_ref):
    normed = norm_ref[...]
    shape = out_ref.shape[2:]
    out_ref[0, 0] = dot_tn(normed, dgate_ref[...]).astype(BF16).reshape(shape)
    out_ref[1, 0] = dot_tn(normed, dup_ref[...]).astype(BF16).reshape(shape)
    out_ref[2, 0] = dot_tn(feed_ref[...], hidden_ref[...]).astype(BF16).reshape(shape)


def attend_back_kernel(
    grad_ref, residual_ref, mine_ref, other_ref, gain_ref, weight_ref,
    query_ref, key_ref, value_ref, prob_ref,
    grad_one, gain_grad, attn_ref, dquery_ref, dkey_ref, dvalue_ref, part_ref, offset_ref,
    dmixed_ref,
):
    step = pl.program_id(0)

    @pl.when(step == 0)
    def _():
        residual = residual_ref[...]
        second = mine_ref[...] + other_ref[...]
        back, gain = norm_back(residual, inverse_rms(residual), gain_ref[1:2, :], second)
        gain_grad[...] = gain
        total = grad_ref[...] + back
        grad_one[...] = total
        lowered = total.astype(BF16)
        attn_ref[...] = lowered
        dmixed_ref[...] = dot(lowered, matrix(weight_ref, 3 * ROWS)).astype(BF16)
        offset_ref[...] = jnp.zeros_like(offset_ref)

    queries = pair_columns(query_ref, step)
    keys = pair_columns(key_ref, step)
    values = pair_columns(value_ref, step)
    dmixed = pair_columns(dmixed_ref, step)
    lanes = lax.broadcasted_iota(jnp.int32, (SLOT, PAIR), 1) // HEAD_DIM
    parts = []
    for which in range(2):
        dprob = dot_nt(jnp.where(lanes == which, dmixed, jnp.zeros_like(dmixed)), values)
        probabilities = prob_ref[which]
        share = jnp.sum(probabilities * dprob, axis=-1, keepdims=True)
        dscore = (probabilities * (dprob - share)).astype(BF16)
        parts.append(
            (
                dot(dscore, keys),
                dot_tn(dscore, queries),
                dot_tn(probabilities.astype(BF16), dmixed),
            )
        )
        offset_ref[pl.ds(2 * step + which, 1), :] = diagonals(dscore.astype(F32))
    for out, first, second in zip((dquery_ref, dkey_ref, dvalue_ref), *parts):
        columns = pl.ds(pl.multiple_of(step * PAIR, PAIR), PAIR)
        out[:, columns] = jnp.where(lanes == 0, first, second).astype(BF16)

    @pl.when(step == pl.num_programs(0) - 1)
    def _():
        part_ref[...] = (
            dot_nt(dquery_ref[...], matrix(weight_ref, 0))
            + dot_nt(dkey_ref[...], matrix(weight_ref, ROWS))
            + dot_nt(dvalue_ref[...], matrix(weight_ref, 2 * ROWS))
        ).astype(BF16)


def square_grads_kernel(norm_ref, attn_ref, mixed_ref, dquery_ref, dkey_ref, dvalue_ref, out_ref):
    normed = norm_ref[...]
    shape = (ROWS,) + out_ref.shape[1:]
    for i, ref in enumerate((dquery_ref, dkey_ref, dvalue_ref)):
        out_ref[i * ROWS : (i + 1) * ROWS] = dot_tn(normed, ref[...]).astype(BF16).reshape(shape)
    out_ref[3 * ROWS :] = dot_tn(attn_ref[...], mixed_ref[...]).astype(BF16).reshape(shape)


def token_grad_kernel(tokens_ref, grad_ref, mine_ref, other_ref, gain_ref, out_ref, gain_grad):
    inputs = tokens_ref[...].astype(F32)
    first = mine_ref[...].astype(F32) + other_ref[...].astype(F32)
    back, gain = norm_back(inputs, inverse_rms(inputs), gain_ref[0:1, :], first)
    out_ref[...] = grad_ref[...] + back
    gain_grad[...] = gain


def order_small_kernel(devices, where_ref, strays_ref, out_ref):
    line = devices // 4
    me = where_ref[0]
    for rz in range(line):
        z = ring_device((ring_place(me // 4, line) - rz + line) % line, line)
        for near in range(4):
            other = z * 4 + jnp.bitwise_xor(me % 4, near)
            out_ref[other] = strays_ref[rz, near].astype(F32)


def stray_update_kernel(own, devices, where_ref, weight, first, second, stray, extra, *refs):
    outs = refs[-4:]
    slot = pl.program_id(0)
    index = where_ref[1] + slot
    grad = jnp.where(index < devices, stray[0].astype(F32), extra[0].astype(F32))
    grad = jnp.where(slot < where_ref[2], grad, 0.0)
    update_slot(weight, first, second, grad, outs)


def update_slot(weight, first, second, grad, outs):
    new_weight, new_first, new_second = adamw_step(
        weight[0], first[0], second[0], grad, RATE_MATRIX
    )
    outs[0][0] = new_weight
    outs[1][0] = new_first
    outs[2][0] = new_second
    outs[3][0] = new_weight.astype(BF16)


def own_update_kernel(where_ref, weight, first, second, grad_ref, *refs):
    outs = refs[-4:]
    grad = jnp.where(pl.program_id(0) < where_ref[4], grad_ref[0], 0.0)
    update_slot(weight, first, second, grad, outs)


def shards(
    tokens,
    out_grad,
    doc_lengths,
    owner_list,
    bucket_table,
    unit_weight,
    unit_first,
    unit_second,
    gain_weight,
    gain_first,
    gain_second,
    bias_weight,
    bias_first,
    bias_second,
    proj_weight,
    proj_first,
    proj_second,
):
    most, _, width = unit_weight.shape
    heads = bias_weight.shape[1]
    count = tokens.shape[0]
    units = owner_list.shape[0]
    proj_width = proj_weight.shape[1]
    devices = lax.axis_size("dp")
    line = devices // 4
    own = max(1, (units - 1) // devices)
    slots = own + 1
    along_x, along_y, along_z = hops(devices)
    me = lax.axis_index("dp").astype(jnp.int32)

    full, left = divmod(units, most)
    stray_most = full * (most - own) + max(0, left - own)
    extra_count = max(0, stray_most - devices)
    indices = jnp.arange(units, dtype=jnp.int32)
    same = owner_list[:, None] == owner_list[None, :]
    rank = jnp.sum((same & (indices[None, :] < indices[:, None])).astype(jnp.int32), axis=1)
    device_ids = jnp.arange(devices, dtype=jnp.int32)
    owned = jnp.sum((owner_list[None, :] == device_ids[:, None]).astype(jnp.int32), axis=1)
    is_stray = rank >= own
    before = (owner_list[None, :] < owner_list[:, None]) & is_stray[None, :]
    stray_index = jnp.sum(before.astype(jnp.int32), axis=1) + rank - own
    position = jnp.where(
        is_stray,
        jnp.where(stray_index < devices, stray_index * slots + own, devices * slots + stray_index - devices),
        owner_list * slots + rank,
    )
    position_ids = jnp.arange(devices * slots + max(extra_count, 1), dtype=jnp.int32)
    hit = position[None, :] == position_ids[:, None]
    placed = jnp.sum(jnp.where(hit, unit_place(indices)[None, :], 0), axis=1)
    table = jnp.where(jnp.any(hit, axis=1), placed, units).astype(jnp.int32)
    my_count = jnp.sum((owner_list == me).astype(jnp.int32))
    my_first = jnp.sum(((owner_list < me) & is_stray).astype(jnp.int32))
    stray_total = jnp.sum(is_stray.astype(jnp.int32))
    where = jnp.stack(
        [me, my_first, jnp.maximum(my_count - own, 0), jnp.maximum(stray_total - devices, 0), my_count]
    ).astype(jnp.int32)
    many = stray_total > devices

    lower = [unit_weight[:own, :HALF].astype(BF16)]
    upper = [unit_weight[:own, HALF:].astype(BF16)]
    for _ in range(line - 1):
        lower.append(send(lower[-1], along_z))
        upper.append(send(upper[-1], along_z))
    pieces = []
    for low, high in zip(lower, upper):
        low_y, high_x = send(low, along_y), send(high, along_x)
        low_x, high_y = send(low, along_x), send(high, along_y)
        low_xy, high_xy = send(low_y, along_x), send(high_x, along_y)
        pieces += [low, high, low_x, high_x, low_y, high_y, low_xy, high_xy]

    half_shape = jax.ShapeDtypeStruct((2, line, HALF, width), BF16)
    keep_a, send_a, keep_b, send_b = pl.pallas_call(
        functools.partial(strays_kernel, own, most, devices),
        out_shape=[half_shape] * 4,
        in_specs=[SMEM, ANY],
        out_specs=[VMEM] * 4,
        scratch_shapes=[
            pltpu.VMEM((most - own, UROWS, width), F32),
            pltpu.SemaphoreType.DMA,
        ],
        compiler_params=params(40),
    )(where, unit_weight)

    def gather_near(values):
        wide = jnp.stack([values, send(values, along_x)])
        return jnp.concatenate([wide, send(wide, along_y)])

    def gather_strays(values):
        near = [gather_near(values)]
        for _ in range(line - 1):
            near.append(send(near[-1], along_z))
        return jnp.stack(near)

    def sum_strays(keep_low, send_low, keep_high, send_high):
        from_x = send(send_low, along_x)
        from_y = send(send_high, along_y)
        low_y = send((keep_low[1].astype(F32) + from_x[1].astype(F32)).astype(BF16), along_y)
        high_x = send((keep_high[1].astype(F32) + from_y[1].astype(F32)).astype(BF16), along_x)
        low = keep_low[0].astype(F32) + from_x[0].astype(F32) + low_y.astype(F32)
        high = keep_high[0].astype(F32) + from_y[0].astype(F32) + high_x.astype(F32)
        summed = jnp.concatenate([low, high], axis=1)
        moving = summed[line - 1]
        for rz in range(line - 2, -1, -1):
            moving = summed[rz] + send(moving.astype(BF16), along_z).astype(F32)
        return moving.astype(BF16)

    strays = gather_strays(sum_strays(keep_a, send_a, keep_b, send_b))

    extra_shape = (max(extra_count, 1), UROWS, width)
    extra_ids = devices + jnp.arange(extra_shape[0], dtype=jnp.int32)

    def extra_weights():
        slot = extra_ids - my_first + own
        mine = (slot >= own) & (slot < my_count)
        taken = jnp.take(unit_weight, jnp.clip(slot, 0, most - 1), axis=0)
        return lax.psum(jnp.where(mine[:, None, None], taken, 0.0), "dp").astype(BF16)

    def no_extra():
        return jnp.zeros(extra_shape, BF16)

    extra = lax.cond(many, extra_weights, no_extra) if extra_count else no_extra()

    stack = pl.pallas_call(
        functools.partial(assemble_kernel, own, devices, units, extra_count),
        out_shape=jax.ShapeDtypeStruct((units + 1, UROWS, width), BF16),
        in_specs=[SMEM, SMEM] + [ANY] * (len(pieces) + 2),
        out_specs=ANY,
        scratch_shapes=[pltpu.SemaphoreType.DMA, pltpu.SemaphoreType.DMA],
        compiler_params=params(16),
    )(where, table, *pieces, strays, extra)

    bucket_hot = (bucket_table[:, None] == jnp.arange(BUCKETS, dtype=jnp.int32)[None, :]).astype(F32)
    bucket_hot = jnp.pad(bucket_hot, ((0, SPREAD - bucket_hot.shape[0]), (0, 0)))
    bias_rows = jnp.pad(precise_dot(bucket_hot, bias_weight).T, ((0, 8 - heads % 8), (0, 0)))
    proj_low = proj_weight.astype(BF16)
    proj_other = swap(proj_low)
    cot_other = swap(out_grad)

    def whole(shape):
        return pl.BlockSpec(shape, lambda i: (0,) * len(shape))

    wide_shape = (count, D)
    head_shape = (count, width)
    square_spec = whole((SQUARES, UROWS, width))
    prob_spec = pl.BlockSpec((2, SLOT, SLOT), lambda i: (i, 0, 0))
    gain_spec = whole((3, D))
    bias_spec = whole(bias_rows.shape)
    column_spec = pl.BlockSpec((count, width), lambda i: (0, i))

    def unit_spec(which):
        return pl.BlockSpec((ROWS, UROWS, width), lambda i: (SQUARES // ROWS + which * BLOCKS + i, 0, 0))

    wide_specs = [unit_spec(0), unit_spec(1), unit_spec(2)]

    def like(shape, kind=F32):
        return jax.ShapeDtypeStruct(shape, kind)

    first_in, queries, keys, values, probabilities, mixed, attn_part = pl.pallas_call(
        attend_kernel,
        grid=(heads // 2,),
        in_specs=[SMEM, whole(wide_shape), gain_spec, square_spec, bias_spec],
        out_specs=[whole(wide_shape)] + [whole(head_shape)] * 3 + [prob_spec, whole(head_shape), whole(wide_shape)],
        out_shape=[like(wide_shape, BF16)]
        + [like(head_shape, BF16)] * 3
        + [like((heads, SLOT, SLOT)), like(head_shape, BF16), like(wide_shape)],
        compiler_params=params(56),
        cost_estimate=cost(8 * count * D * width, 12e6, heads * SLOT * SLOT),
    )(doc_lengths, tokens, gain_weight, stack, bias_rows)

    residual_one, second_in, gate, up, hidden, feed_part = pl.pallas_call(
        feed_kernel,
        grid=(BLOCKS,),
        in_specs=[whole(wide_shape)] * 3 + [gain_spec] + wide_specs,
        out_specs=[whole(wide_shape)] * 2 + [column_spec] * 3 + [whole(wide_shape)],
        out_shape=[
            like(wide_shape),
            like(wide_shape, BF16),
            like((count, BLOCKS * width)),
            like((count, BLOCKS * width)),
            like((count, BLOCKS * width), BF16),
            like(wide_shape),
        ],
        compiler_params=params(56),
        cost_estimate=cost(6 * count * D * BLOCKS * width, 24e6),
    )(tokens, attn_part, swap(attn_part), gain_weight, stack, stack, stack)

    encoded, proj_grad, gain_three, grad_two, feed_grad, dgate, dup, second_part = pl.pallas_call(
        turn_kernel,
        grid=(BLOCKS,),
        in_specs=[SMEM]
        + [whole(wide_shape)] * 3
        + [gain_spec]
        + [whole((D, proj_width))] * 2
        + [whole((count, proj_width))] * 2
        + [column_spec] * 2
        + wide_specs,
        out_specs=[
            whole((count, proj_width)),
            whole((2, proj_width, D // 2)),
            whole((1, D)),
            whole(wide_shape),
            whole(wide_shape),
            column_spec,
            column_spec,
            whole(wide_shape),
        ],
        out_shape=[
            like((count, proj_width)),
            like((2, proj_width, D // 2)),
            like((1, D)),
            like(wide_shape),
            like(wide_shape, BF16),
            like((count, BLOCKS * width), BF16),
            like((count, BLOCKS * width), BF16),
            like(wide_shape),
        ],
        compiler_params=params(56),
        cost_estimate=cost(6 * count * D * BLOCKS * width, 24e6),
    )(
        doc_lengths, residual_one, feed_part, swap(feed_part), gain_weight, proj_low, proj_other,
        out_grad, cot_other, gate, up, stack, stack, stack,
    )

    wides = pl.pallas_call(
        wide_grads_kernel,
        grid=(BLOCKS,),
        in_specs=[whole(wide_shape)] * 2 + [column_spec] * 3,
        out_specs=pl.BlockSpec((3, 1, ROWS, UROWS, width), lambda i: (0, i, 0, 0, 0)),
        out_shape=like((3, BLOCKS, ROWS, UROWS, width), BF16),
        compiler_params=params(56),
        cost_estimate=cost(6 * count * D * BLOCKS * width, 12e6),
    )(second_in, feed_grad, hidden, dgate, dup)
    wides = wides.reshape(3 * BLOCKS * ROWS, UROWS, width)

    grad_one, gain_two, attn_grad, dquery, dkey, dvalue, first_part, offset_grad = pl.pallas_call(
        attend_back_kernel,
        grid=(heads // 2,),
        in_specs=[whole(wide_shape)] * 4 + [gain_spec, square_spec] + [whole(head_shape)] * 3 + [prob_spec],
        out_specs=[whole(wide_shape), whole((1, D)), whole(wide_shape)]
        + [whole(head_shape)] * 3
        + [whole(wide_shape), bias_spec],
        out_shape=[like(wide_shape), like((1, D)), like(wide_shape, BF16)]
        + [like(head_shape, BF16)] * 3
        + [like(wide_shape, BF16), like(bias_rows.shape)],
        scratch_shapes=[pltpu.VMEM(head_shape, BF16)],
        compiler_params=params(56),
        cost_estimate=cost(10 * count * D * width, 16e6),
    )(
        grad_two, residual_one, second_part, swap(second_part), gain_weight, stack,
        queries, keys, values, probabilities,
    )

    squares = pl.pallas_call(
        square_grads_kernel,
        out_shape=like((SQUARES, UROWS, width), BF16),
        compiler_params=params(56),
        cost_estimate=cost(8 * count * D * width, 6e6),
    )(first_in, attn_grad, mixed, dquery, dkey, dvalue)

    token_grad, gain_one = pl.pallas_call(
        token_grad_kernel,
        out_shape=[like(wide_shape), like((1, D))],
        compiler_params=params(56),
        cost_estimate=cost(20 * count * D, 6e6),
    )(tokens, grad_one, first_part, swap(first_part), gain_weight)

    bias_grad = precise_dot(bucket_hot.T, offset_grad[:heads].T)
    gain_rows = jnp.concatenate([gain_one, gain_two, gain_three]).reshape(-1, width)
    bias_row = jnp.pad(bias_grad.reshape(1, -1), ((0, 0), (0, width - BUCKETS * heads)))
    proj_rows = proj_grad.reshape(-1, width)
    small = jnp.concatenate([proj_rows, gain_rows, bias_row])
    share = -(-small.shape[0] // devices)
    small = jnp.pad(small, ((0, share * devices - small.shape[0]), (0, 0)))
    small = small.reshape(devices, share, width)
    small = jnp.pad(small, ((0, 0), (0, SMALL_TILE - share), (0, 0))).astype(BF16)

    part_shape = like((2, own, HALF, width), BF16)
    stray_low = like((2, line, HALF, width), BF16)
    stray_high = like((2, line, HALF + SMALL_TILE, width), BF16)
    spread = pl.pallas_call(
        functools.partial(spread_kernel, own, devices, units),
        out_shape=[part_shape] * (4 * line) + [stray_low] * 2 + [stray_high] * 2,
        in_specs=[SMEM, SMEM, ANY, ANY, ANY],
        out_specs=[ANY] * (4 * line + 4),
        scratch_shapes=[pltpu.SemaphoreType.DMA, pltpu.SemaphoreType.DMA],
        compiler_params=params(16),
    )(where, table, squares, wides, small)

    stray_grads = gather_strays(sum_strays(*spread[4 * line :]))

    moving = None
    for rz in range(line - 1, -1, -1):
        keep_a, send_a, keep_b, send_b = spread[4 * rz : 4 * rz + 4]
        from_x = send(send_a, along_x)
        from_y = send(send_b, along_y)
        low_y = send((keep_a[1].astype(F32) + from_x[1].astype(F32)).astype(BF16), along_y)
        high_x = send((keep_b[1].astype(F32) + from_y[1].astype(F32)).astype(BF16), along_x)
        low = keep_a[0].astype(F32) + from_x[0].astype(F32) + low_y.astype(F32)
        high = keep_b[0].astype(F32) + from_y[0].astype(F32) + high_x.astype(F32)
        summed = jnp.concatenate([low, high], axis=1)
        if moving is not None:
            summed = summed + send(moving.astype(BF16), along_z).astype(F32)
        moving = summed
    own_grads = moving

    def extra_grads():
        every = jnp.concatenate([squares, wides]).astype(F32)
        taken = jnp.take(every, jnp.minimum(table[devices * slots :], units - 1), axis=0)
        return lax.psum(taken, "dp").astype(BF16)

    extra_grad = lax.cond(many, extra_grads, no_extra) if extra_count else no_extra()

    def near_place(index):
        z = ring_place(index // 4, line)
        rz = (ring_place(me // 4, line) - z + line) % line
        return rz * 4 + jnp.bitwise_xor(index % 4, me % 4)

    stray_ids = jnp.minimum(my_first + jnp.arange(most - own, dtype=jnp.int32), devices - 1)
    extra_picks = jnp.clip(my_first + jnp.arange(most - own, dtype=jnp.int32) - devices, 0, extra_shape[0] - 1)
    picks = jnp.concatenate([where, near_place(stray_ids), extra_picks])
    head = where.shape[0]

    def slot_spec(first):
        return pl.BlockSpec((1, UROWS, width), lambda i, pick: (first + i, 0, 0))

    stack_shape = unit_weight.shape
    update_shapes = [like(stack_shape)] * 3 + [like(stack_shape, BF16)]
    partial_update = pl.pallas_call(
        functools.partial(stray_update_kernel, own, devices),
        grid_spec=pltpu.PrefetchScalarGridSpec(
            num_scalar_prefetch=1,
            grid=(most - own,),
            in_specs=[slot_spec(own)] * 3
            + [
                pl.BlockSpec((1, UROWS, width), lambda i, pick: (pick[head + i], 0, 0)),
                pl.BlockSpec((1, UROWS, width), lambda i, pick: (pick[head + most - own + i], 0, 0)),
            ],
            out_specs=[slot_spec(own)] * 4,
        ),
        out_shape=update_shapes,
        compiler_params=params(32),
        cost_estimate=cost(1e7, 10e6),
    )(picks, unit_weight, unit_first, unit_second, stray_grads.reshape(devices, -1, width), extra_grad)
    unit_weights, unit_firsts, unit_seconds, unit_copies = pl.pallas_call(
        own_update_kernel,
        grid_spec=pltpu.PrefetchScalarGridSpec(
            num_scalar_prefetch=1,
            grid=(own,),
            in_specs=[slot_spec(0)] * 4 + [ANY] * 4,
            out_specs=[slot_spec(0)] * 4,
        ),
        out_shape=update_shapes,
        input_output_aliases={5: 0, 6: 1, 7: 2, 8: 3},
        compiler_params=params(32),
        cost_estimate=cost(1e7, 6e6),
    )(where, unit_weight, unit_first, unit_second, own_grads, *partial_update)

    small_total = pl.pallas_call(
        functools.partial(order_small_kernel, devices),
        out_shape=like((devices, SMALL_TILE, width)),
        in_specs=[SMEM, VMEM],
        compiler_params=params(32),
    )(where, stray_grads[:, :, UROWS:])
    small_total = small_total[:, :share].reshape(devices * share, width)
    proj_count = proj_rows.shape[0]
    proj_total = small_total[:proj_count].reshape(2, proj_width, D // 2)
    proj_total = proj_total.transpose(0, 2, 1).reshape(D, proj_width)
    gain_total = small_total[proj_count : proj_count + gain_rows.shape[0]].reshape(3, D)
    bias_total = small_total[proj_count + gain_rows.shape[0], : BUCKETS * heads].reshape(BUCKETS, heads)
    gain_weights, gain_firsts, gain_seconds = adamw_step(
        gain_weight, gain_first, gain_second, gain_total, RATE_GAIN
    )
    bias_weights, bias_firsts, bias_seconds = adamw_step(
        bias_weight, bias_first, bias_second, bias_total, RATE_SMALL
    )
    proj_weights, proj_firsts, proj_seconds = adamw_step(
        proj_weight, proj_first, proj_second, proj_total, RATE_MATRIX
    )
    return (
        encoded,
        token_grad,
        unit_weights,
        unit_firsts,
        unit_seconds,
        unit_copies,
        gain_weights,
        gain_firsts,
        gain_seconds,
        bias_weights,
        bias_firsts,
        bias_seconds,
        proj_weights,
        proj_firsts,
        proj_seconds,
    )


def solution(mesh):
    in_specs = (
        P("dp", None),
        P("dp", "mp"),
        P("dp"),
        P(),
        P(),
        P("dp", None, "mp"),
        P("dp", None, "mp"),
        P("dp", None, "mp"),
        P(),
        P(),
        P(),
        P(None, "mp"),
        P(None, "mp"),
        P(None, "mp"),
        P(None, "mp"),
        P(None, "mp"),
        P(None, "mp"),
    )
    out_specs = (
        P("dp", "mp"),
        P("dp", None),
        P("dp", None, "mp"),
        P("dp", None, "mp"),
        P("dp", None, "mp"),
        P("dp", None, "mp"),
        P(),
        P(),
        P(),
        P(None, "mp"),
        P(None, "mp"),
        P(None, "mp"),
        P(None, "mp"),
        P(None, "mp"),
        P(None, "mp"),
    )
    return jax.shard_map(shards, mesh=mesh, in_specs=in_specs, out_specs=out_specs, check_vma=False)
```

time: 2820 us -> 471 us (0.17)
  other arithmetic: 1460 us -> 21.1 us
  local copies, waits for them, and re-layouts: 1130 us -> 47 us
  Pallas kernels: 0 us -> 128 us
  starting transfers between devices: 1.14 us -> 117 us
  waiting for transfers between devices: 57.2 us -> 144 us
  blocking collectives: 74.7 us -> 0 us
  matrix products: 59 us -> 0.6 us
    scatter-add x1 -> x0, other arithmetic: 1390 us -> none  [shards(): jax.ops.segment_sum(score_total.reshape(local_heads, SLOT * SLOT).T, rela...]
    gather x4 -> x0, local copies, waits for them, and re-layouts: 981 us -> none  [the longest x2 934 us: shards(): score_bias = jnp.take(by_offset.T, relative, axis=1)]
    ppermute x0 -> x79, waiting for transfers between devices: none -> 144 us  [the longest x73 134 us: send(): return lax.ppermute(values, 'dp', pairs)]
    pallas_call x0 -> x13, Pallas kernels: none -> 128 us  [the longest x1 28.6 us: shards(): pl.pallas_call(functools.partial(spread_kernel, own, devices, units), out...]
    ppermute x0 -> x79, starting transfers between devices: none -> 117 us  [the longest x73 116 us: send(): return lax.ppermute(values, 'dp', pairs)]
    psum x1 -> x0, blocking collectives: 74.7 us -> none  [shards(): lax.psum((jnp.stack([gain_one, gain_two, gain_three]), bias_grad, proj_gr...]
    transpose x3 -> x0, local copies, waits for them, and re-layouts: 62.4 us -> none  [the longest x2 62.1 us: shards(): score_total.reshape(local_heads, SLOT * SLOT)]
    dot_general x32 -> x2, matrix products: 59 us -> 0.6 us  [precise_dot(): jnp.dot(left, right, precision=lax.Precision.HIGHEST, preferred_element_t...]
  transfers between devices with their start and end apart: 7 -> 79, of which waited for: 4 -> 37; matrix products, arithmetic and copies ran while one was open for 91% -> 5% of each run, Pallas kernels for 0% -> 3%
where the time goes in v1:
time: 471 us; the launch traced here: 462 us
  waiting for transfers between devices  144 us (31%)
  Pallas kernels  128 us (27%)
  starting transfers between devices  117 us (25%)
  local copies, waits for them, and re-layouts  47 us (10%)
  other arithmetic  21.1 us (4%)
    ppermute x73, waiting for transfers between devices, send(): return lax.ppermute(values, 'dp', pairs)  134 us
    ppermute x73, starting transfers between devices, send(): return lax.ppermute(values, 'dp', pairs)  116 us
    unnamed x123, local copies, waits for them, and re-layouts  29.8 us
    pallas_call x1, Pallas kernels, shards(): pl.pallas_call(functools.partial(spread_kernel, own, devices, units), out...  28.6 us
    pallas_call x1, Pallas kernels, shards(): pl.pallas_call(attend_back_kernel, grid=(heads // 2,), in_specs=[whole(wi...  17 us
    pallas_call x1, Pallas kernels, shards(): pl.pallas_call(turn_kernel, grid=(BLOCKS,), in_specs=[SMEM] + [whole(wide...  14 us
    pallas_call x1, Pallas kernels, shards(): pl.pallas_call(attend_kernel, grid=(heads // 2,), in_specs=[SMEM, whole(w...  12.7 us
    pallas_call x1, Pallas kernels, shards(): pl.pallas_call(functools.partial(assemble_kernel, own, devices, units, ex...  11.8 us
  transfers between devices with their start and end apart: 79, of which 37 were waited for; matrix products, arithmetic and copies ran while one was open for 5% of the time, Pallas kernels for 3%

profile of v1, /device:TPU:0, one launch (start us, length us, event | category | flops | bytes accessed | tf_op | source)
XLA Modules:
  0.0 461.7 jit_solution(3113296911370530745)
XLA Ops:
  8.5 3.1 collective-permute-start.30
  13.1 7.6 %collective-permute-done.30 = bf16[2,4,64,384]{3,2,1,0:T(8,128)(2,1)S(1)} collective-permute-done((bf16[2,4,64,384]{3,2,1,0:T(8,128)(2,1)S(1)}, bf16[2,4,64,384]{3,2,1,0:T(8,128)(2,1)S(1)}, u32[]{:S(2)}, u32[]{:S(2)}) %collective-permute-start.30) | collective-permute-done | bytes 393248 | tf_op jit(solution)/shard_map/ppermute | solution.py:114
  24.2 2.7 collective-permute-done.31
  28.4 2.9 collective-permute-start.34
  33.6 3.4 collective-permute-start.35
  39.8 3.4 collective-permute-start.36
  48.5 3.7 collective-permute-done.7.refs_9_
  59.0 3.2 collective-permute-start.9
  70.5 2.9 collective-permute-start.39
  75.5 2.8 collective-permute-start.4
  82.9 3.4 collective-permute-start.40
  92.1 4.0 collective-permute-done.40
  96.1 3.4 collective-permute-start.41
  124.9 11.8 %shard_map.281.weight_ref.gate_w.up_w.down_w = bf16[97,128,384]{2,1,0:T(8,128)(2,1)S(1)} custom-call(s32[5]{0:T(128)S(1)} %stack.71.where_ref, s32[136]{0:T(256)S(1)} %broadcast_select_fusion.1.table_ref, bf16[5,64,384]{2,1,0:T(8,128)(2,1)S(1)} %get-tuple-element.249.refs_0_, bf16[5,64,384]{2,1,0:T(8,128)(2,1)S(1)} %get-tuple-element.248.refs_1_, ...), custom_call_target="tpu_custom_call" | custom-call | tf_op jit(solution)/shard_map/pallas_call | solution.py:631
  136.7 3.7 copy-done
  140.4 12.7 %shard_map.282 = (bf16[512,768]{1,0:T(8,128)(2,1)}, bf16[512,384]{1,0:T(8,128)(2,1)}, bf16[512,384]{1,0:T(8,128)(2,1)}, bf16[512,384]{1,0:T(8,128)(2,1)}, f32[6,...) custom-call(s32[1]{0:T(128)S(6)} %copy.88.lengths_ref, bf16[512,768]{1,0:T(8,128)(2,1)} %tokens_ref.5, ...), custom_call_target="tpu_custom_call" | custom-call | flops 1207959552 | bytes 12000000 | tf_op jit(solution)/shard_map/pallas_call | solution.py:666
  153.3 3.6 collective-permute-done.42.other_ref
  158.0 11.5 %shard_map.283 = (f32[512,768]{1,0:T(8,128)}, bf16[512,768]{1,0:T(8,128)(2,1)}, f32[512,1536]{1,0:T(8,128)}, f32[512,1536]{1,0:T(8,128)}, bf16[512,1536]{1,0:T(8,128)(2,1)}, /*index=5*/f32[512,768]{1,0:T(8,128)}) custom-call(bf16[512,768]{1,0:T(8,128)(2,1)} %tokens_ref.5, f32[512,768]{1,0:T(8,128)} %get-tuple-element.112.mine_ref, f32[512,768]{1,0:T(8,128)} %copy-done.40, ...), custom_call_target="tpu_custom_call" | custom-call | flops 3623878656 | bytes 24000000 | tf_op jit(solution)/shard_map/pallas_call | solution.py:678
  170.7 2.8 collective-permute-done.45.cot_other
  174.8 14.0 %shard_map.284 = (f32[512,64]{1,0:T(8,128)}, f32[2,64,384]{2,1,0:T(8,128)}, f32[1,768]{1,0:T(1,128)}, f32[512,768]{1,0:T(8,128)}, bf16[512,768]{1,0:T(8,128)(2,1...) custom-call(s32[1]{0:T(128)S(6)} %copy.88.lengths_ref, ...), custom_call_target="tpu_custom_call" | custom-call | flops 3623878656 | bytes 24000000 | tf_op jit(solution)/shard_map/pallas_call | solution.py:695
  189.0 3.5 collective-permute-done.46.other_ref
  193.6 17.0 %shard_map.285 = (f32[512,768]{1,0:T(8,128)}, f32[1,768]{1,0:T(1,128)}, bf16[512,768]{1,0:T(8,128)(2,1)}, bf16[512,384]{1,0:T(8,128)(2,1)}, bf16[512,384]{1,0:T(...) custom-call(f32[512,768]{1,0:T(8,128)} %get-tuple-element.118.grad_ref, ...), custom_call_target="tpu_custom_call" | custom-call | flops 1509949440 | bytes 16000000 | tf_op jit(solution)/shard_map/pallas_call | solution.py:743
  210.9 9.4 %shard_map.288 = bf16[3,4,6,128,384]{4,3,2,1,0:T(8,128)(2,1)} custom-call(bf16[512,768]{1,0:T(8,128)(2,1)} %get-tuple-element.133.norm_ref, bf16[512,768]{1,0:T(8,128)(2,1)} %get-tuple-element.134.feed_ref, bf16[512,1536]{1,0:T(8,128)(2,1)} %get-tuple-element.135.hidden_ref, bf16[512,1536]{1,0:T(8,128)(2,1)} %get-tuple-element.136.dgate_ref, ...), custom_call_target="tpu_custom_call" | custom-call | flops 3623878656 | bytes 12000000 | tf_op jit(solution)/shard_map/pallas_call | solution.py:732
  220.8 5.1 %shard_map.287.squares_ref = bf16[24,128,384]{2,1,0:T(8,128)(2,1)} custom-call(bf16[512,768]{1,0:T(8,128)(2,1)} %get-tuple-element.127.norm_ref, bf16[512,768]{1,0:T(8,128)(2,1)} %get-tuple-element.128.attn_ref, bf16[512,384]{1,0:T(8,128)(2,1)} %get-tuple-element.129.mixed_ref, bf16[512,384]{1,0:T(8,128)(2,1)} %get-tuple-element.130.dquery_ref, ...), custom_call_target="tpu_custom_call" | custom-call | flops 1207959552 | bytes 6000000 | tf_op jit(solution)/shard_map/pallas_call | solution.py:761
  226.8 4.1 shard_map.286
  231.7 28.6 %shard_map.289 = (bf16[2,5,64,384]{3,2,1,0:T(8,128)(2,1)S(1)}, bf16[2,5,64,384]{3,2,1,0:T(8,128)(2,1)}, bf16[2,5,64,384]{3,2,1,0:T(8,128)(2,1)S(1)}, bf16[2,5,64...) custom-call(s32[5]{0:T(128)S(1)} %stack.71.where_ref, ...), custom_call_target="tpu_custom_call" | custom-call | tf_op jit(solution)/shard_map/pallas_call | solution.py:788
  276.8 2.8 conditional.3
  283.6 8.2 %collective-permute-done.48 = bf16[2,5,64,384]{3,2,1,0:T(8,128)(2,1)} collective-permute-done((bf16[2,5,64,384]{3,2,1,0:T(8,128)(2,1)}, bf16[2,5,64,384]{3,2,1,0:T(8,128)(2,1)}, u32[]{:S(2)}, u32[]{:S(2)}) %collective-permute-start.48) | collective-permute-done | bytes 491552 | tf_op jit(solution)/shard_map/ppermute | solution.py:114
  295.9 6.3 %collective-permute-done.52 = bf16[2,5,64,384]{3,2,1,0:T(8,128)(2,1)S(1)} collective-permute-done((bf16[2,5,64,384]{3,2,1,0:T(8,128)(2,1)}, bf16[2,5,64,384]{3,2,1,0:T(8,128)(2,1)S(1)}, u32[]{:S(2)}, u32[]{:S(2)}) %collective-permute-start.52) | collective-permute-done | bytes 491552 | tf_op jit(solution)/shard_map/ppermute | solution.py:114
  304.5 8.3 %collective-permute-done.56 = bf16[2,5,64,384]{3,2,1,0:T(8,128)(2,1)S(1)} collective-permute-done((bf16[2,5,64,384]{3,2,1,0:T(8,128)(2,1)}, bf16[2,5,64,384]{3,2,1,0:T(8,128)(2,1)S(1)}, u32[]{:S(2)}, u32[]{:S(2)}) %collective-permute-start.56) | collective-permute-done | bytes 491552 | tf_op jit(solution)/shard_map/ppermute | solution.py:114
  315.0 7.7 %collective-permute-done.60 = bf16[2,5,64,384]{3,2,1,0:T(8,128)(2,1)S(1)} collective-permute-done((bf16[2,5,64,384]{3,2,1,0:T(8,128)(2,1)}, bf16[2,5,64,384]{3,2,1,0:T(8,128)(2,1)S(1)}, u32[]{:S(2)}, u32[]{:S(2)}) %collective-permute-start.60) | collective-permute-done | bytes 491552 | tf_op jit(solution)/shard_map/ppermute | solution.py:114
  333.8 4.0 collective-permute-done.70
  339.8 7.6 %collective-permute-done.57 = bf16[5,64,384]{2,1,0:T(8,128)(2,1)S(1)} collective-permute-done((bf16[5,64,384]{2,1,0:T(8,128)(2,1)S(1)}, bf16[5,64,384]{2,1,0:T(8,128)(2,1)S(1)}, u32[]{:S(2)}, u32[]{:S(2)}) %collective-permute-start.57) | collective-permute-done | bytes 245792 | tf_op jit(solution)/shard_map/ppermute | solution.py:114
  348.7 3.1 collective-permute-done.61
  353.2 3.3 collective-permute-done.71
  363.0 2.9 collective-permute-start.73
  366.0 3.4 collective-permute-done.73
  369.3 3.4 collective-permute-start.64
  373.6 4.0 collective-permute-done.74
  380.2 4.8 %collective-permute-done.75 = bf16[2,144,384]{2,1,0:T(8,128)(2,1)S(1)} collective-permute-done((bf16[2,144,384]{2,1,0:T(8,128)(2,1)S(1)}, bf16[2,144,384]{2,1,0:T(8,128)(2,1)S(1)}, u32[]{:S(2)}, u32[]{:S(2)}) %collective-permute-start.75) | collective-permute-done | bytes 221216 | tf_op jit(solution)/shard_map/ppermute | solution.py:114
  385.0 3.4 collective-permute-start.65
  388.7 17.1 %collective-permute-done.76 = bf16[4,144,384]{2,1,0:T(8,128)(2,1)S(1)} collective-permute-done((bf16[4,144,384]{2,1,0:T(8,128)(2,1)S(1)}, bf16[4,144,384]{2,1,0:T(8,128)(2,1)S(1)}, u32[]{:S(2)}, u32[]{:S(2)}) %collective-permute-start.76) | collective-permute-done | bytes 442400 | tf_op jit(solution)/shard_map/ppermute | solution.py:114
  405.9 3.4 collective-permute-start.77
  410.5 9.4 %collective-permute-done.77 = bf16[4,144,384]{2,1,0:T(8,128)(2,1)S(1)} collective-permute-done((bf16[4,144,384]{2,1,0:T(8,128)(2,1)S(1)}, bf16[4,144,384]{2,1,0:T(8,128)(2,1)S(1)}, u32[]{:S(2)}, u32[]{:S(2)}) %collective-permute-start.77) | collective-permute-done | bytes 442400 | tf_op jit(solution)/shard_map/ppermute | solution.py:114
  419.9 3.4 collective-permute-start.78
  426.7 4.7 %collective-permute-done.78 = bf16[4,144,384]{2,1,0:T(8,128)(2,1)S(1)} collective-permute-done((bf16[4,144,384]{2,1,0:T(8,128)(2,1)S(1)}, bf16[4,144,384]{2,1,0:T(8,128)(2,1)S(1)}, u32[]{:S(2)}, u32[]{:S(2)}) %collective-permute-start.78) | collective-permute-done | bytes 442400 | tf_op jit(solution)/shard_map/ppermute | solution.py:114
  450.4 7.4 %shard_map.290 = (f32[13,128,384]{2,1,0:T(8,128)}, f32[13,128,384]{2,1,0:T(8,128)}, f32[13,128,384]{2,1,0:T(8,128)}, bf16[13,128,384]{2,1,0:T(8,128)(2,1)}) custom-call(s32[21]{0:T(128)S(1)} %concatenate.50.where_ref, f32[13,128,384]{2,1,0:T(8,128)} %weight.3, f32[13,128,384]{2,1,0:T(8,128)S(1)} %copy-done.1, f32[13,128,384]{2,1,0:T(8,128)S(1)} %copy-done.2, ...), custom_call_target="tpu_custom_call" | custom-call | flops 10000000 | bytes 10000000 | tf_op jit(solution)/shard_map/pallas_call | solution.py:836
  457.9 3.4 shard_map.291
  (334 shorter events, 166.2 us)
Async XLA Ops:
  8.5 12.2 %collective-permute-start.30 = (bf16[2,4,64,384]{3,2,1,0:T(8,128)(2,1)S(1)}, bf16[2,4,64,384]{3,2,1,0:T(8,128)(2,1)S(1)}, u32[]{:S(2)}, u32[]{:S(2)}) collective-permute-start(bf16[2,4,64,384]{3,2,1,0:T(8,128)(2,1)S(1)} %get-tuple-element.109), channel_id=1, source_target_pairs={{0,2},{2,0},{4,6},{6,4},{8,10},{10,8},{12,14},{14,12},{16,18},{18,... | collective-permute-start | bytes 1179656 | tf_op jit(solution)/shard_map/ppermute | solution.py:114
  11.6 10.9 %collective-permute-start.32 = (bf16[2,4,64,384]{3,2,1,0:T(8,128)(2,1)S(1)}, bf16[2,4,64,384]{3,2,1,0:T(8,128)(2,1)S(1)}, u32[]{:S(2)}, u32[]{:S(2)}) collective-permute-start(bf16[2,4,64,384]{3,2,1,0:T(8,128)(2,1)S(1)} %get-tuple-element.111), channel_id=1, source_target_pairs={{0,4},{2,6},{4,0},{6,2},{8,12},{10,14},{12,8},{14,10},{16,20},{18,... | collective-permute-start | bytes 1179656 | tf_op jit(solution)/shard_map/ppermute | solution.py:114
  43.9 9.5 %collective-permute-start.3 = (bf16[5,64,384]{2,1,0:T(8,128)(2,1)S(1)}, bf16[5,64,384]{2,1,0:T(8,128)(2,1)S(1)}, u32[]{:S(2)}, u32[]{:S(2)}) collective-permute-start(bf16[5,64,384]{2,1,0:T(8,128)(2,1)S(1)} %get-tuple-element.248.refs_1_), channel_id=1, source_target_pairs={{0,4},{2,6},{4,0},{6,2},{8,12},{10,14},{12,8},{14,10},{16,20},{18,... | collective-permute-start | bytes 737288 | tf_op jit(solution)/shard_map/ppermute | solution.py:114
  45.9 12.2 %collective-permute-start.6 = (bf16[5,64,384]{2,1,0:T(8,128)(2,1)S(1)}, bf16[5,64,384]{2,1,0:T(8,128)(2,1)S(1)}, u32[]{:S(2)}, u32[]{:S(2)}) collective-permute-start(bf16[5,64,384]{2,1,0:T(8,128)(2,1)S(1)} %get-tuple-element.249.refs_0_), channel_id=1, source_target_pairs={{0,16},{2,18},{4,20},{6,22},{8,0},{10,2},{12,4},{14,6},{16,24},{18... | collective-permute-start | bytes 737288 | tf_op jit(solution)/shard_map/ppermute | solution.py:114
  53.9 11.0 %collective-permute-start.15 = (bf16[5,64,384]{2,1,0:T(8,128)(2,1)S(1)}, bf16[5,64,384]{2,1,0:T(8,128)(2,1)S(1)}, u32[]{:S(2)}, u32[]{:S(2)}) collective-permute-start(bf16[5,64,384]{2,1,0:T(8,128)(2,1)S(1)} %collective-permute-done.7.refs_9_), channel_id=1, source_target_pairs={{0,16},{2,18},{4,20},{6,22},{8,0},{10,2},{12,4},{14,6},{16,24},{18... | collective-permute-start | bytes 737288 | tf_op jit(solution)/shard_map/ppermute | solution.py:114
  58.1 10.3 %collective-permute-start.38 = (bf16[2,128,384]{2,1,0:T(8,128)(2,1)S(1)}, bf16[2,128,384]{2,1,0:T(8,128)(2,1)S(1)}, u32[]{:S(2)}, u32[]{:S(2)}) collective-permute-start(bf16[2,128,384]{2,1,0:T(8,128)(2,1)S(1)} %pad_maximum_fusion.8), channel_id=1, source_target_pairs={{0,4},{2,6},{4,0},{6,2},{8,12},{10,14},{12,8},{14,10},{16,20},{18,... | collective-permute-start | bytes 589832 | tf_op jit(solution)/shard_map/ppermute | solution.py:114
  59.0 11.5 %collective-permute-start.9 = (bf16[5,64,384]{2,1,0:T(8,128)(2,1)S(1)}, bf16[5,64,384]{2,1,0:T(8,128)(2,1)S(1)}, u32[]{:S(2)}, u32[]{:S(2)}) collective-permute-start(bf16[5,64,384]{2,1,0:T(8,128)(2,1)S(1)} %collective-permute-done.7.refs_9_), channel_id=1, source_target_pairs={{0,2},{2,0},{4,6},{6,4},{8,10},{10,8},{12,14},{14,12},{16,18},{18,... | collective-permute-start | bytes 737288 | tf_op jit(solution)/shard_map/ppermute | solution.py:114
  62.2 16.1 %collective-permute-start.14 = (bf16[5,64,384]{2,1,0:T(8,128)(2,1)S(1)}, bf16[5,64,384]{2,1,0:T(8,128)(2,1)S(1)}, u32[]{:S(2)}, u32[]{:S(2)}) collective-permute-start(bf16[5,64,384]{2,1,0:T(8,128)(2,1)S(1)} %collective-permute-done.6.refs_8_), channel_id=1, source_target_pairs={{0,16},{2,18},{4,20},{6,22},{8,0},{10,2},{12,4},{14,6},{16,24},{18... | collective-permute-start | bytes 737288 | tf_op jit(solution)/shard_map/ppermute | solution.py:114
  64.9 15.9 %collective-permute-start.10 = (bf16[5,64,384]{2,1,0:T(8,128)(2,1)S(1)}, bf16[5,64,384]{2,1,0:T(8,128)(2,1)S(1)}, u32[]{:S(2)}, u32[]{:S(2)}) collective-permute-start(bf16[5,64,384]{2,1,0:T(8,128)(2,1)S(1)} %collective-permute-done.6.refs_8_), channel_id=1, source_target_pairs={{0,4},{2,6},{4,0},{6,2},{8,12},{10,14},{12,8},{14,10},{16,20},{18,... | collective-permute-start | bytes 737288 | tf_op jit(solution)/shard_map/ppermute | solution.py:114
  64.9 16.7 %collective-permute-start.8 = (bf16[5,64,384]{2,1,0:T(8,128)(2,1)S(1)}, bf16[5,64,384]{2,1,0:T(8,128)(2,1)S(1)}, u32[]{:S(2)}, u32[]{:S(2)}) collective-permute-start(bf16[5,64,384]{2,1,0:T(8,128)(2,1)S(1)} %collective-permute-done.6.refs_8_), channel_id=1, source_target_pairs={{0,2},{2,0},{4,6},{6,4},{8,10},{10,8},{12,14},{14,12},{16,18},{18,... | collective-permute-start | bytes 737288 | tf_op jit(solution)/shard_map/ppermute | solution.py:114
  70.5 12.4 %collective-permute-start.39 = (bf16[4,128,384]{2,1,0:T(8,128)(2,1)S(1)}, bf16[4,128,384]{2,1,0:T(8,128)(2,1)S(1)}, u32[]{:S(2)}, u32[]{:S(2)}) collective-permute-start(bf16[4,128,384]{2,1,0:T(8,128)(2,1)S(1)} %get-tuple-element.253), channel_id=1, source_target_pairs={{0,16},{2,18},{4,20},{6,22},{8,0},{10,2},{12,4},{14,6},{16,24},{18... | collective-permute-start | bytes 1179656 | tf_op jit(solution)/shard_map/ppermute | solution.py:114
  75.5 10.8 %collective-permute-start.4 = (bf16[5,64,384]{2,1,0:T(8,128)(2,1)S(1)}, bf16[5,64,384]{2,1,0:T(8,128)(2,1)S(1)}, u32[]{:S(2)}, u32[]{:S(2)}) collective-permute-start(bf16[5,64,384]{2,1,0:T(8,128)(2,1)S(1)} %collective-permute-done.2.refs_4_), channel_id=1, source_target_pairs={{0,2},{2,0},{4,6},{6,4},{8,10},{10,8},{12,14},{14,12},{16,18},{18,... | collective-permute-start | bytes 737288 | tf_op jit(solution)/shard_map/ppermute | solution.py:114
  78.3 9.8 %collective-permute-start.23 = (bf16[5,64,384]{2,1,0:T(8,128)(2,1)S(1)}, bf16[5,64,384]{2,1,0:T(8,128)(2,1)S(1)}, u32[]{:S(2)}, u32[]{:S(2)}) collective-permute-start(bf16[5,64,384]{2,1,0:T(8,128)(2,1)S(1)} %collective-permute-done.15.refs_17_), channel_id=1, source_target_pairs={{0,16},{2,18},{4,20},{6,22},{8,0},{10,2},{12,4},{14,6},{16,24},{18... | collective-permute-start | bytes 737288 | tf_op jit(solution)/shard_map/ppermute | solution.py:114
  81.6 9.9 %collective-permute-start.17 = (bf16[5,64,384]{2,1,0:T(8,128)(2,1)S(1)}, bf16[5,64,384]{2,1,0:T(8,128)(2,1)}, u32[]{:S(2)}, u32[]{:S(2)}) collective-permute-start(bf16[5,64,384]{2,1,0:T(8,128)(2,1)S(1)} %collective-permute-done.15.refs_17_), channel_id=1, source_target_pairs={{0,2},{2,0},{4,6},{6,4},{8,10},{10,8},{12,14},{14,12},{16,18},{18,... | collective-permute-start | bytes 737288 | tf_op jit(solution)/shard_map/ppermute | solution.py:114
  82.9 13.2 %collective-permute-start.40 = (bf16[4,128,384]{2,1,0:T(8,128)(2,1)S(1)}, bf16[4,128,384]{2,1,0:T(8,128)(2,1)S(1)}, u32[]{:S(2)}, u32[]{:S(2)}) collective-permute-start(bf16[4,128,384]{2,1,0:T(8,128)(2,1)S(1)} %collective-permute-done.39), channel_id=1, source_target_pairs={{0,16},{2,18},{4,20},{6,22},{8,0},{10,2},{12,4},{14,6},{16,24},{18... | collective-permute-start | bytes 1179656 | tf_op jit(solution)/shard_map/ppermute | solution.py:114
  87.0 16.4 %collective-permute-start.22 = (bf16[5,64,384]{2,1,0:T(8,128)(2,1)S(1)}, bf16[5,64,384]{2,1,0:T(8,128)(2,1)}, u32[]{:S(2)}, u32[]{:S(2)}) collective-permute-start(bf16[5,64,384]{2,1,0:T(8,128)(2,1)S(1)} %collective-permute-done.14.refs_16_), channel_id=1, source_target_pairs={{0,16},{2,18},{4,20},{6,22},{8,0},{10,2},{12,4},{14,6},{16,24},{18... | collective-permute-start | bytes 737288 | tf_op jit(solution)/shard_map/ppermute | solution.py:114
  88.1 17.4 %collective-permute-start.18 = (bf16[5,64,384]{2,1,0:T(8,128)(2,1)S(1)}, bf16[5,64,384]{2,1,0:T(8,128)(2,1)}, u32[]{:S(2)}, u32[]{:S(2)}) collective-permute-start(bf16[5,64,384]{2,1,0:T(8,128)(2,1)S(1)} %collective-permute-done.14.refs_16_), channel_id=1, source_target_pairs={{0,4},{2,6},{4,0},{6,2},{8,12},{10,14},{12,8},{14,10},{16,20},{18,... | collective-permute-start | bytes 737288 | tf_op jit(solution)/shard_map/ppermute | solution.py:114
  89.8 16.5 %collective-permute-start.16 = (bf16[5,64,384]{2,1,0:T(8,128)(2,1)S(1)}, bf16[5,64,384]{2,1,0:T(8,128)(2,1)S(1)}, u32[]{:S(2)}, u32[]{:S(2)}) collective-permute-start(bf16[5,64,384]{2,1,0:T(8,128)(2,1)S(1)} %collective-permute-done.14.refs_16_), channel_id=1, source_target_pairs={{0,2},{2,0},{4,6},{6,4},{8,10},{10,8},{12,14},{14,12},{16,18},{18,... | collective-permute-start | bytes 737288 | tf_op jit(solution)/shard_map/ppermute | solution.py:114
  96.1 20.7 %collective-permute-start.41 = (bf16[4,128,384]{2,1,0:T(8,128)(2,1)S(1)}, bf16[4,128,384]{2,1,0:T(8,128)(2,1)S(1)}, u32[]{:S(2)}, u32[]{:S(2)}) collective-permute-start(bf16[4,128,384]{2,1,0:T(8,128)(2,1)S(1)} %collective-permute-done.40), channel_id=1, source_target_pairs={{0,16},{2,18},{4,20},{6,22},{8,0},{10,2},{12,4},{14,6},{16,24},{18... | collective-permute-start | bytes 1179656 | tf_op jit(solution)/shard_map/ppermute | solution.py:114
  105.5 9.8 %collective-permute-start.25 = (bf16[5,64,384]{2,1,0:T(8,128)(2,1)S(1)}, bf16[5,64,384]{2,1,0:T(8,128)(2,1)}, u32[]{:S(2)}, u32[]{:S(2)}) collective-permute-start(bf16[5,64,384]{2,1,0:T(8,128)(2,1)S(1)} %collective-permute-done.23.refs_25_), channel_id=1, source_target_pairs={{0,2},{2,0},{4,6},{6,4},{8,10},{10,8},{12,14},{14,12},{16,18},{18,... | collective-permute-start | bytes 737288 | tf_op jit(solution)/shard_map/ppermute | solution.py:114
  109.8 14.9 %collective-permute-start.24 = (bf16[5,64,384]{2,1,0:T(8,128)(2,1)}, bf16[5,64,384]{2,1,0:T(8,128)(2,1)}, u32[]{:S(2)}, u32[]{:S(2)}) collective-permute-start(bf16[5,64,384]{2,1,0:T(8,128)(2,1)} %collective-permute-done.22.refs_24_), channel_id=1, source_target_pairs={{0,2},{2,0},{4,6},{6,4},{8,10},{10,8},{12,14},{14,12},{16,18},{18,... | collective-permute-start | bytes 737288 | tf_op jit(solution)/shard_map/ppermute | solution.py:114
  112.9 11.7 %collective-permute-start.21 = (bf16[5,64,384]{2,1,0:T(8,128)(2,1)}, bf16[5,64,384]{2,1,0:T(8,128)(2,1)}, u32[]{:S(2)}, u32[]{:S(2)}) collective-permute-start(bf16[5,64,384]{2,1,0:T(8,128)(2,1)} %collective-permute-done.17.refs_19_), channel_id=1, source_target_pairs={{0,4},{2,6},{4,0},{6,2},{8,12},{10,14},{12,8},{14,10},{16,20},{18,... | collective-permute-start | bytes 737288 | tf_op jit(solution)/shard_map/ppermute | solution.py:114
  210.6 15.2 %collective-permute-start.47 = (bf16[512,768]{1,0:T(8,128)(2,1)}, bf16[512,768]{1,0:T(8,128)(2,1)S(1)}, u32[]{:S(2)}, u32[]{:S(2)}) collective-permute-start(bf16[512,768]{1,0:T(8,128)(2,1)} %get-tuple-element.125.mine_ref), channel_id=1, source_target_pairs={{0,1},{1,0},{2,3},{3,2},{4,5},{5,4},{6,7},{7,6},{8,9},{9,8},{10,11... | collective-permute-start | bytes 2359304 | tf_op jit(solution)/shard_map/ppermute | solution.py:118
  269.0 12.2 %collective-permute-start.67 = (bf16[2,4,64,384]{3,2,1,0:T(8,128)(2,1)}, bf16[2,4,64,384]{3,2,1,0:T(8,128)(2,1)}, u32[]{:S(2)}, u32[]{:S(2)}) collective-permute-start(bf16[2,4,64,384]{3,2,1,0:T(8,128)(2,1)} %get-tuple-element.160), channel_id=1, source_target_pairs={{0,2},{2,0},{4,6},{6,4},{8,10},{10,8},{12,14},{14,12},{16,18},{18,... | collective-permute-start | bytes 1179656 | tf_op jit(solution)/shard_map/ppermute | solution.py:114
  270.3 21.5 %collective-permute-start.48 = (bf16[2,5,64,384]{3,2,1,0:T(8,128)(2,1)}, bf16[2,5,64,384]{3,2,1,0:T(8,128)(2,1)}, u32[]{:S(2)}, u32[]{:S(2)}) collective-permute-start(bf16[2,5,64,384]{3,2,1,0:T(8,128)(2,1)} %get-tuple-element.144), channel_id=1, source_target_pairs={{0,2},{2,0},{4,6},{6,4},{8,10},{10,8},{12,14},{14,12},{16,18},{18,... | collective-permute-start | bytes 1474568 | tf_op jit(solution)/shard_map/ppermute | solution.py:114
  271.0 23.8 %collective-permute-start.50 = (bf16[2,5,64,384]{3,2,1,0:T(8,128)(2,1)}, bf16[2,5,64,384]{3,2,1,0:T(8,128)(2,1)}, u32[]{:S(2)}, u32[]{:S(2)}) collective-permute-start(bf16[2,5,64,384]{3,2,1,0:T(8,128)(2,1)} %copy-done.36), channel_id=1, source_target_pairs={{0,4},{2,6},{4,0},{6,2},{8,12},{10,14},{12,8},{14,10},{16,20},{18,... | collective-permute-start | bytes 1474568 | tf_op jit(solution)/shard_map/ppermute | solution.py:114
  279.6 22.6 %collective-permute-start.52 = (bf16[2,5,64,384]{3,2,1,0:T(8,128)(2,1)}, bf16[2,5,64,384]{3,2,1,0:T(8,128)(2,1)S(1)}, u32[]{:S(2)}, u32[]{:S(2)}) collective-permute-start(bf16[2,5,64,384]{3,2,1,0:T(8,128)(2,1)} %copy-done.35), channel_id=1, source_target_pairs={{0,2},{2,0},{4,6},{6,4},{8,10},{10,8},{12,14},{14,12},{16,18},{18,... | collective-permute-start | bytes 1474568 | tf_op jit(solution)/shard_map/ppermute | solution.py:114
  279.7 24.6 %collective-permute-start.54 = (bf16[2,5,64,384]{3,2,1,0:T(8,128)(2,1)}, bf16[2,5,64,384]{3,2,1,0:T(8,128)(2,1)S(1)}, u32[]{:S(2)}, u32[]{:S(2)}) collective-permute-start(bf16[2,5,64,384]{3,2,1,0:T(8,128)(2,1)} %copy-done.34), channel_id=1, source_target_pairs={{0,4},{2,6},{4,0},{6,2},{8,12},{10,14},{12,8},{14,10},{16,20},{18,... | collective-permute-start | bytes 1474568 | tf_op jit(solution)/shard_map/ppermute | solution.py:114
  281.2 31.5 %collective-permute-start.56 = (bf16[2,5,64,384]{3,2,1,0:T(8,128)(2,1)}, bf16[2,5,64,384]{3,2,1,0:T(8,128)(2,1)S(1)}, u32[]{:S(2)}, u32[]{:S(2)}) collective-permute-start(bf16[2,5,64,384]{3,2,1,0:T(8,128)(2,1)} %copy-done.33), channel_id=1, source_target_pairs={{0,2},{2,0},{4,6},{6,4},{8,10},{10,8},{12,14},{14,12},{16,18},{18,... | collective-permute-start | bytes 1474568 | tf_op jit(solution)/shard_map/ppermute | solution.py:114
  291.8 23.0 %collective-permute-start.58 = (bf16[2,5,64,384]{3,2,1,0:T(8,128)(2,1)}, bf16[2,5,64,384]{3,2,1,0:T(8,128)(2,1)S(1)}, u32[]{:S(2)}, u32[]{:S(2)}) collective-permute-start(bf16[2,5,64,384]{3,2,1,0:T(8,128)(2,1)} %copy-done.32), channel_id=1, source_target_pairs={{0,4},{2,6},{4,0},{6,2},{8,12},{10,14},{12,8},{14,10},{16,20},{18,... | collective-permute-start | bytes 1474568 | tf_op jit(solution)/shard_map/ppermute | solution.py:114
  294.8 27.9 %collective-permute-start.60 = (bf16[2,5,64,384]{3,2,1,0:T(8,128)(2,1)}, bf16[2,5,64,384]{3,2,1,0:T(8,128)(2,1)S(1)}, u32[]{:S(2)}, u32[]{:S(2)}) collective-permute-start(bf16[2,5,64,384]{3,2,1,0:T(8,128)(2,1)} %copy-done.31), channel_id=1, source_target_pairs={{0,2},{2,0},{4,6},{6,4},{8,10},{10,8},{12,14},{14,12},{16,18},{18,... | collective-permute-start | bytes 1474568 | tf_op jit(solution)/shard_map/ppermute | solution.py:114
  302.2 21.9 %collective-permute-start.62 = (bf16[2,5,64,384]{3,2,1,0:T(8,128)(2,1)}, bf16[2,5,64,384]{3,2,1,0:T(8,128)(2,1)S(1)}, u32[]{:S(2)}, u32[]{:S(2)}) collective-permute-start(bf16[2,5,64,384]{3,2,1,0:T(8,128)(2,1)} %copy-done.30), channel_id=1, source_target_pairs={{0,4},{2,6},{4,0},{6,2},{8,12},{10,14},{12,8},{14,10},{16,20},{18,... | collective-permute-start | bytes 1474568 | tf_op jit(solution)/shard_map/ppermute | solution.py:114
  304.3 23.2 %collective-permute-start.69 = (bf16[2,4,80,384]{3,2,1,0:T(8,128)(2,1)S(1)}, bf16[2,4,80,384]{3,2,1,0:T(8,128)(2,1)S(1)}, u32[]{:S(2)}, u32[]{:S(2)}) collective-permute-start(bf16[2,4,80,384]{3,2,1,0:T(8,128)(2,1)S(1)} %copy-done.29), channel_id=1, source_target_pairs={{0,4},{2,6},{4,0},{6,2},{8,12},{10,14},{12,8},{14,10},{16,20},{18,... | collective-permute-start | bytes 1474568 | tf_op jit(solution)/shard_map/ppermute | solution.py:114
  312.7 18.9 %collective-permute-start.68 = (bf16[4,64,384]{2,1,0:T(8,128)(2,1)S(1)}, bf16[4,64,384]{2,1,0:T(8,128)(2,1)S(1)}, u32[]{:S(2)}, u32[]{:S(2)}) collective-permute-start(bf16[4,64,384]{2,1,0:T(8,128)(2,1)S(1)} %fusion.32), channel_id=1, source_target_pairs={{0,4},{2,6},{4,0},{6,2},{8,12},{10,14},{12,8},{14,10},{16,20},{18,... | collective-permute-start | bytes 589832 | tf_op jit(solution)/shard_map/ppermute | solution.py:114
  314.8 94.6 %collective-permute-start.49 = (bf16[5,64,384]{2,1,0:T(8,128)(2,1)S(1)}, bf16[5,64,384]{2,1,0:T(8,128)(2,1)S(1)}, u32[]{:S(2)}, u32[]{:S(2)}) collective-permute-start(bf16[5,64,384]{2,1,0:T(8,128)(2,1)S(1)} %fusion.6), channel_id=1, source_target_pairs={{0,4},{2,6},{4,0},{6,2},{8,12},{10,14},{12,8},{14,10},{16,20},{18,... | collective-permute-start | bytes 737288 | tf_op jit(solution)/shard_map/ppermute | solution.py:114
  322.7 100.5 %collective-permute-start.51 = (bf16[5,64,384]{2,1,0:T(8,128)(2,1)S(1)}, bf16[5,64,384]{2,1,0:T(8,128)(2,1)S(1)}, u32[]{:S(2)}, u32[]{:S(2)}) collective-permute-start(bf16[5,64,384]{2,1,0:T(8,128)(2,1)S(1)} %fusion.7), channel_id=1, source_target_pairs={{0,2},{2,0},{4,6},{6,4},{8,10},{10,8},{12,14},{14,12},{16,18},{18,... | collective-permute-start | bytes 737288 | tf_op jit(solution)/shard_map/ppermute | solution.py:114
  324.1 64.4 %collective-permute-start.53 = (bf16[5,64,384]{2,1,0:T(8,128)(2,1)S(1)}, bf16[5,64,384]{2,1,0:T(8,128)(2,1)S(1)}, u32[]{:S(2)}, u32[]{:S(2)}) collective-permute-start(bf16[5,64,384]{2,1,0:T(8,128)(2,1)S(1)} %fusion.8), channel_id=1, source_target_pairs={{0,4},{2,6},{4,0},{6,2},{8,12},{10,14},{12,8},{14,10},{16,20},{18,... | collective-permute-start | bytes 737288 | tf_op jit(solution)/shard_map/ppermute | solution.py:114
  327.5 20.0 %collective-permute-start.57 = (bf16[5,64,384]{2,1,0:T(8,128)(2,1)S(1)}, bf16[5,64,384]{2,1,0:T(8,128)(2,1)S(1)}, u32[]{:S(2)}, u32[]{:S(2)}) collective-permute-start(bf16[5,64,384]{2,1,0:T(8,128)(2,1)S(1)} %fusion.10), channel_id=1, source_target_pairs={{0,4},{2,6},{4,0},{6,2},{8,12},{10,14},{12,8},{14,10},{16,20},{18,... | collective-permute-start | bytes 737288 | tf_op jit(solution)/shard_map/ppermute | solution.py:114
  337.9 13.9 %collective-permute-start.61 = (bf16[5,64,384]{2,1,0:T(8,128)(2,1)S(1)}, bf16[5,64,384]{2,1,0:T(8,128)(2,1)S(1)}, u32[]{:S(2)}, u32[]{:S(2)}) collective-permute-start(bf16[5,64,384]{2,1,0:T(8,128)(2,1)S(1)} %fusion.12), channel_id=1, source_target_pairs={{0,4},{2,6},{4,0},{6,2},{8,12},{10,14},{12,8},{14,10},{16,20},{18,... | collective-permute-start | bytes 737288 | tf_op jit(solution)/shard_map/ppermute | solution.py:114
  347.5 10.1 %collective-permute-start.63 = (bf16[5,64,384]{2,1,0:T(8,128)(2,1)S(1)}, bf16[5,64,384]{2,1,0:T(8,128)(2,1)S(1)}, u32[]{:S(2)}, u32[]{:S(2)}) collective-permute-start(bf16[5,64,384]{2,1,0:T(8,128)(2,1)S(1)} %fusion.13), channel_id=1, source_target_pairs={{0,2},{2,0},{4,6},{6,4},{8,10},{10,8},{12,14},{14,12},{16,18},{18,... | collective-permute-start | bytes 737288 | tf_op jit(solution)/shard_map/ppermute | solution.py:114
  356.5 16.2 %collective-permute-start.59 = (bf16[5,64,384]{2,1,0:T(8,128)(2,1)S(1)}, bf16[5,64,384]{2,1,0:T(8,128)(2,1)S(1)}, u32[]{:S(2)}, u32[]{:S(2)}) collective-permute-start(bf16[5,64,384]{2,1,0:T(8,128)(2,1)S(1)} %fusion.11), channel_id=1, source_target_pairs={{0,2},{2,0},{4,6},{6,4},{8,10},{10,8},{12,14},{14,12},{16,18},{18,... | collective-permute-start | bytes 737288 | tf_op jit(solution)/shard_map/ppermute | solution.py:114
  369.3 9.7 %collective-permute-start.64 = (bf16[5,128,384]{2,1,0:T(8,128)(2,1)S(1)}, bf16[5,128,384]{2,1,0:T(8,128)(2,1)S(1)}, u32[]{:S(2)}, u32[]{:S(2)}) collective-permute-start(bf16[5,128,384]{2,1,0:T(8,128)(2,1)S(1)} %pad_maximum_fusion.2), channel_id=1, source_target_pairs={{0,16},{2,18},{4,20},{6,22},{8,0},{10,2},{12,4},{14,6},{16,24},{18... | collective-permute-start | bytes 1474568 | tf_op jit(solution)/shard_map/ppermute | solution.py:114
  377.6 11.1 %collective-permute-start.55 = (bf16[5,64,384]{2,1,0:T(8,128)(2,1)S(1)}, bf16[5,64,384]{2,1,0:T(8,128)(2,1)S(1)}, u32[]{:S(2)}, u32[]{:S(2)}) collective-permute-start(bf16[5,64,384]{2,1,0:T(8,128)(2,1)S(1)} %fusion.9), channel_id=1, source_target_pairs={{0,2},{2,0},{4,6},{6,4},{8,10},{10,8},{12,14},{14,12},{16,18},{18,... | collective-permute-start | bytes 737288 | tf_op jit(solution)/shard_map/ppermute | solution.py:114
  385.0 24.2 %collective-permute-start.65 = (bf16[5,128,384]{2,1,0:T(8,128)(2,1)S(1)}, bf16[5,128,384]{2,1,0:T(8,128)(2,1)S(1)}, u32[]{:S(2)}, u32[]{:S(2)}) collective-permute-start(bf16[5,128,384]{2,1,0:T(8,128)(2,1)S(1)} %fusion.1), channel_id=1, source_target_pairs={{0,16},{2,18},{4,20},{6,22},{8,0},{10,2},{12,4},{14,6},{16,24},{18... | collective-permute-start | bytes 1474568 | tf_op jit(solution)/shard_map/ppermute | solution.py:114
  388.5 17.4 %collective-permute-start.76 = (bf16[4,144,384]{2,1,0:T(8,128)(2,1)S(1)}, bf16[4,144,384]{2,1,0:T(8,128)(2,1)S(1)}, u32[]{:S(2)}, u32[]{:S(2)}) collective-permute-start(bf16[4,144,384]{2,1,0:T(8,128)(2,1)S(1)} %get-tuple-element.251), channel_id=1, source_target_pairs={{0,16},{2,18},{4,20},{6,22},{8,0},{10,2},{12,4},{14,6},{16,24},{18... | collective-permute-start | bytes 1327112 | tf_op jit(solution)/shard_map/ppermute | solution.py:114
  405.9 14.0 %collective-permute-start.77 = (bf16[4,144,384]{2,1,0:T(8,128)(2,1)S(1)}, bf16[4,144,384]{2,1,0:T(8,128)(2,1)S(1)}, u32[]{:S(2)}, u32[]{:S(2)}) collective-permute-start(bf16[4,144,384]{2,1,0:T(8,128)(2,1)S(1)} %collective-permute-done.76), channel_id=1, source_target_pairs={{0,16},{2,18},{4,20},{6,22},{8,0},{10,2},{12,4},{14,6},{16,24},{18... | collective-permute-start | bytes 1327112 | tf_op jit(solution)/shard_map/ppermute | solution.py:114
  409.4 17.2 %collective-permute-start.66 = (bf16[5,128,384]{2,1,0:T(8,128)(2,1)S(1)}, bf16[5,128,384]{2,1,0:T(8,128)(2,1)S(1)}, u32[]{:S(2)}, u32[]{:S(2)}) collective-permute-start(bf16[5,128,384]{2,1,0:T(8,128)(2,1)S(1)} %fusion), channel_id=1, source_target_pairs={{0,16},{2,18},{4,20},{6,22},{8,0},{10,2},{12,4},{14,6},{16,24},{18... | collective-permute-start | bytes 1474568 | tf_op jit(solution)/shard_map/ppermute | solution.py:114
  419.9 11.5 %collective-permute-start.78 = (bf16[4,144,384]{2,1,0:T(8,128)(2,1)S(1)}, bf16[4,144,384]{2,1,0:T(8,128)(2,1)S(1)}, u32[]{:S(2)}, u32[]{:S(2)}) collective-permute-start(bf16[4,144,384]{2,1,0:T(8,128)(2,1)S(1)} %collective-permute-done.77), channel_id=1, source_target_pairs={{0,16},{2,18},{4,20},{6,22},{8,0},{10,2},{12,4},{14,6},{16,24},{18... | collective-permute-start | bytes 1327112 | tf_op jit(solution)/shard_map/ppermute | solution.py:114
  (91 other events, 769.6 us)
